TPU v7x, 512 devices: a whole 4x4x16 slice. The times are simulated.
512 devices in a mesh: dp: 32 (over x, z_hi, core), mp: 16 (over y, z_lo).
Axes of the slice: x: 4, y: 4, z: 16 (z_hi: 4, z_lo: 4; z = z_hi * 4 + z_lo), core: 2. Of those that a mesh axis runs over, the one named last changes fastest.
Arguments:
- pool: bfloat16 [256, 32, 5120], P('dp', None, 'mp'), may hold values from -20 to 20
- send_table: int32 [32, 32], P('dp'), may hold values from -1 to 7, as said below
- slot_source: int32 [256], P('dp'), may hold values from 0 to 31, as said below
- multiplicity: int32 [256], P('dp'), may hold values from 1 to 4
- slot_weight: float32 [256], P('dp'), may hold values from 0.1 to 1
- cotangent: bfloat16 [256, 32, 4096], P('dp', None, 'mp'), may hold values from -6 to 6
- w_query: bfloat16 [5120, 4096], P(None, 'mp'), may hold values from -0.078125 to 0.078125
- w_key: bfloat16 [5120, 512], P('mp'), may hold values from -0.078125 to 0.078125
- w_value: bfloat16 [5120, 512], P('mp'), may hold values from -0.078125 to 0.078125
- query_gain: float32 [128], replicated, may hold values from 0.5 to 5
- key_gain: float32 [128], replicated, may hold values from 0.5 to 5
Outputs:
- attended: bfloat16 [256, 32, 4096], P('dp', None, 'mp')
- grad_query: float32 [5120, 4096], P('dp', 'mp')
- key_gradient: float32 [5120, 512], P('mp', 'dp')
- grad_value: float32 [5120, 512], P('mp', 'dp')
Inputs may be any that keep to these rules, and one draw needn't show every extreme that they name: Entry [r, d] is the sequence of rank r's pool of 8 that data rank d receives from rank r, or -1 where rank d takes nothing from rank r; send_table[r, d] >= 0 exactly where r is among the sources of rank d's slots. `slot_source`: the 8 slots of data rank d (entries d * 8 to d * 8 + 7) name 8 different source ranks.
All inputs are finite; a program needn't handle non-finite values.
Results may differ from a plain program's by a relative error of at most 0.025.
The roundings to bfloat16 on the way count: a program that leaves them out, or rounds other values in their place, can miss the bound.
Values may be sent and summed in bfloat16 or wider, within the bound.
A program may use at most 64 MiB of HBM per device.

v0:
```python
import math

import jax
import jax.numpy as jnp
from jax import lax
from jax.sharding import PartitionSpec as P

HEADS = 32
KV_HEADS = 4


def rms_scale(values, gain):
    inverse = lax.rsqrt(jnp.mean(values * values, axis=-1, keepdims=True) + 1e-06)
    return (values * inverse * gain, inverse)


def rms_back(values, inverse, gain, grad_out):
    scaled = grad_out * gain
    inner = jnp.mean(values * scaled, axis=-1, keepdims=True)
    return inverse * scaled - values * (inverse * inverse * inverse) * inner


def forward_core(query, key_sum, value_sum, query_gain, key_gain):
    scale = 1.0 / math.sqrt(query.shape[-1])
    q_norm, q_inverse = rms_scale(query, query_gain)
    k_norm, k_inverse = rms_scale(key_sum, key_gain)
    q_half = q_norm.astype(jnp.bfloat16)
    k_half = k_norm.astype(jnp.bfloat16)
    v_half = value_sum.astype(jnp.bfloat16)
    score_matrix = (
        jnp.einsum("sqgph,skgh->sgpqk", q_half, k_half, preferred_element_type=jnp.float32) * scale
    )
    length = query.shape[1]
    causal = lax.broadcasted_iota(jnp.int32, (length, length), 0) >= lax.broadcasted_iota(
        jnp.int32, (length, length), 1
    )
    score_matrix = jnp.where(causal, score_matrix, -1e30)
    peak = jnp.max(score_matrix, axis=-1, keepdims=True)
    raised = jnp.exp(score_matrix - peak)
    probs = raised / jnp.sum(raised, axis=-1, keepdims=True)
    p_half = probs.astype(jnp.bfloat16)
    attended = jnp.einsum("sgpqk,skgh->sqgph", p_half, v_half, preferred_element_type=jnp.float32)
    return (attended, (q_inverse, k_inverse, q_half, k_half, v_half, probs, p_half))


def backward_core(d_out, query, key_sum, query_gain, key_gain, saved):
    q_inverse, k_inverse, q_half, k_half, v_half, probs, p_half = saved
    scale = 1.0 / math.sqrt(query.shape[-1])
    out_half = d_out.astype(jnp.bfloat16)
    d_probs = jnp.einsum("sqgph,skgh->sgpqk", out_half, v_half, preferred_element_type=jnp.float32)
    d_value = jnp.einsum("sgpqk,sqgph->skgh", p_half, out_half, preferred_element_type=jnp.float32)
    d_scores = probs * (d_probs - jnp.sum(d_probs * probs, axis=-1, keepdims=True)) * scale
    score_half = d_scores.astype(jnp.bfloat16)
    d_qnorm = jnp.einsum(
        "sgpqk,skgh->sqgph", score_half, k_half, preferred_element_type=jnp.float32
    )
    d_knorm = jnp.einsum(
        "sgpqk,sqgph->skgh", score_half, q_half, preferred_element_type=jnp.float32
    )
    d_query = rms_back(query, q_inverse, query_gain, d_qnorm)
    d_key = rms_back(key_sum, k_inverse, key_gain, d_knorm)
    return (d_query, d_key, d_value)


def local(
    pool,
    send_table,
    slot_source,
    multiplicity,
    slot_weight,
    cotangent,
    w_query,
    w_key,
    w_value,
    query_gain,
    key_gain,
):
    slot_count = slot_source.shape[0]
    length = pool.shape[1]
    local_width = pool.shape[2]
    query_cols = w_query.shape[1]
    key_cols = w_key.shape[1]
    head_dim = query_gain.shape[0]
    heads_here = query_cols // head_dim
    group_size = HEADS // KV_HEADS
    token_count = slot_count * length
    outgoing_index = send_table[0]
    outgoing = jnp.take(pool, jnp.maximum(outgoing_index, 0), axis=0)
    outgoing = jnp.where((outgoing_index >= 0)[:, None, None], outgoing, jnp.zeros_like(outgoing))
    arrived = lax.all_to_all(outgoing, "dp", split_axis=0, concat_axis=0, tiled=True)
    chosen = jnp.take(arrived, slot_source, axis=0)
    local_rows = chosen.reshape(token_count, local_width)
    piece = lax.all_gather(local_rows, "mp", axis=1, tiled=True)
    query_total = jnp.dot(piece, w_query, preferred_element_type=jnp.float32)
    key_part = jnp.dot(local_rows, w_key, preferred_element_type=jnp.float32)
    value_part = jnp.dot(local_rows, w_value, preferred_element_type=jnp.float32)
    group_index = lax.axis_index("mp") * heads_here // group_size
    offset = group_index * head_dim
    key_all, value_all = lax.psum((key_part, value_part), "mp")
    key_own = lax.dynamic_slice_in_dim(key_all, offset, head_dim, 1)
    value_own = lax.dynamic_slice_in_dim(value_all, offset, head_dim, 1)
    key_sum = key_own.reshape(slot_count, length, 1, head_dim)
    value_sum = value_own.reshape(slot_count, length, 1, head_dim)
    query = query_total.reshape(slot_count, length, 1, heads_here, head_dim)
    attended, saved = forward_core(query, key_sum, value_sum, query_gain, key_gain)
    attended_out = attended.reshape(slot_count, length, query_cols).astype(jnp.bfloat16)
    factor = multiplicity.astype(jnp.float32) * slot_weight / length
    d_out = (
        cotangent.astype(jnp.float32).reshape(slot_count, length, 1, heads_here, head_dim)
        * factor[:, None, None, None, None]
    )
    d_query, d_key, d_value = backward_core(d_out, query, key_sum, query_gain, key_gain, saved)
    query_rows = d_query.reshape(token_count, query_cols).astype(jnp.bfloat16)
    blank = jnp.zeros((token_count, key_cols), jnp.float32)
    key_place = lax.dynamic_update_slice_in_dim(
        blank, d_key.reshape(token_count, head_dim), offset, 1
    )
    value_place = lax.dynamic_update_slice_in_dim(
        blank, d_value.reshape(token_count, head_dim), offset, 1
    )
    key_grads, value_grads = (
        lax.psum(key_place.astype(jnp.bfloat16), "mp").astype(jnp.float32),
        lax.psum(value_place.astype(jnp.bfloat16), "mp").astype(jnp.float32),
    )
    key_half = key_grads.astype(jnp.bfloat16)
    value_half = value_grads.astype(jnp.bfloat16)
    key_term = jnp.einsum("td,tc->dc", local_rows, key_half, preferred_element_type=jnp.float32)
    value_term = jnp.einsum("td,tc->dc", local_rows, value_half, preferred_element_type=jnp.float32)
    query_whole = jnp.einsum("td,tc->dc", piece, query_rows, preferred_element_type=jnp.float32)
    grad_query, key_gradient, grad_value = (
        lax.psum_scatter(
            query_whole.astype(jnp.bfloat16), "dp", scatter_dimension=0, tiled=True
        ).astype(jnp.float32),
        lax.psum_scatter(
            key_term.astype(jnp.bfloat16), "dp", scatter_dimension=1, tiled=True
        ).astype(jnp.float32),
        lax.psum_scatter(
            value_term.astype(jnp.bfloat16), "dp", scatter_dimension=1, tiled=True
        ).astype(jnp.float32),
    )
    return (attended_out, grad_query, key_gradient, grad_value)


def solution(mesh):
    return jax.shard_map(
        local,
        mesh=mesh,
        in_specs=(
            P("dp", None, "mp"),
            P("dp", None),
            P("dp"),
            P("dp"),
            P("dp"),
            P("dp", None, "mp"),
            P(None, "mp"),
            P("mp", None),
            P("mp", None),
            P(),
            P(),
        ),
        out_specs=(P("dp", None, "mp"), P("dp", "mp"), P("mp", "dp"), P("mp", "dp")),
        check_vma=False,
    )
```

profile of v0, /device:TPU:1, one launch (start us, length us, event | category | flops | bytes accessed | tf_op | source)
XLA Modules:
  0.0 875.6 jit_solution(9019244908626197756)
XLA Ops:
  7.2 0.8 compare_bitcast_fusion.1
  8.0 0.7 maximum_bitcast_fusion
  8.7 1.6 gather_fusion
  10.3 1.1 select_select_fusion
  11.4 19.3 %all-to-all-start = ((bf16[32,32,320]{2,1,0:T(8,128)(2,1)}), bf16[32,32,320]{2,1,0:T(8,128)(2,1)S(1)}, u32[]{:S(2)}, u32[]{:S(2)}) async-start(bf16[32,32,320]{2,1,0:T(8,128)(2,1)} %select_select_fusion), calls=%async_computation | async-start | bytes 1572864 | tf_op jit(solution)/shard_map/all_to_all | solution.py:90
  31.0 38.6 %all-to-all-done = bf16[32,32,320]{2,1,0:T(8,128)(2,1)S(1)} async-done(((bf16[32,32,320]{2,1,0:T(8,128)(2,1)}), bf16[32,32,320]{2,1,0:T(8,128)(2,1)S(1)}, u32[]{:S(2)}, u32[]{:S(2)}) %all-to-all-start) | async-done | bytes 655392 | tf_op jit(solution)/shard_map/all_to_all | solution.py:90
  69.7 1.2 gather_fusion.1
  70.9 1.0 bitcast_select_fusion
  71.9 2.1 fusion.31
  74.1 0.8 copy.69
  75.0 1.3 fusion.30
  76.3 85.9 %all-reduce.8 = bf16[256,512]{1,0:T(8,128)(2,1)} all-reduce(f32[256,512]{1,0:T(8,128)S(1)} %fusion.30), channel_id=1, replica_groups=mesh['dp'=32,'mp'=16] {'mp'}, use_global_device_ids=true, to_apply=%region_0.1 | all-reduce | flops 131072 | bytes 786432 | tf_op jit(solution)/shard_map/psum | solution.py:99
  162.2 72.2 %all-reduce.5.cloned.1.call-done = f32[256,512]{1,0:T(8,128)} async-done(((f32[256,512]{1,0:T(8,128)}), f32[256,512]{1,0:T(8,128)}) %all-reduce.5.cloned.1.call-update) | async-done | bytes 524304 | tf_op jit(solution)/shard_map/psum | solution.py:99
  234.3 1.0 multiply_reduce_fusion.4
  235.5 96.5 %all-gather.2.cloned.1.call-done = bf16[256,5120]{0,1:T(8,128)(2,1)} async-done(((bf16[256,320]{0,1:T(8,128)(2,1)}), bf16[256,5120]{0,1:T(8,128)(2,1)}) %all-gather.2.cloned.1.call-update) | async-done | bytes 2621456 | tf_op jit(solution)/shard_map/all_gather | solution.py:93
  332.0 3.3 fusion.32
  335.3 1.1 reshape.266
  336.4 1.1 reshape.265
  337.5 1.0 multiply_reduce_fusion.2
  338.5 1.0 copy.70
  339.5 0.6 multiply_multiply_fusion
  340.1 0.4 fusion.29
  340.7 1.1 fusion.15
  341.8 0.9 dynamic-slice_convert_fusion
  342.7 1.0 multiply_reduce_fusion.1
  343.8 0.1 fusion.12
  343.9 1.3 multiply_reduce_fusion.3
  345.2 0.2 multiply_subtract_fusion
  345.4 0.7 broadcast_in_dim.72
  346.1 0.6 constant_dynamic-update-slice_fusion.1
  346.8 169.0 %all-reduce.7.cloned.1.call-done = (bf16[256,512]{1,0:T(8,128)(2,1)}, bf16[256,512]{1,0:T(8,128)(2,1)}) async-done(((bf16[256,512]{1,0:T(8,128)(2,1)}, bf16[256,512]{1,0:T(8,128)(2,1)}), (bf16[256,512]{1,0:T(8,128)(2,1)}, bf16[256,512]{1,0:T(8,128)(2,1)})) %all-reduce.7.cloned.1.call-update) | async-done | bytes 524304 | tf_op jit(solution)/shard_map/psum | solution.py:122
  515.8 2.1 convolution_convert_fusion.1
  517.9 1.7 multiply_reduce_fusion
  519.6 0.7 copy.78
  520.3 2.0 convolution_convert_fusion.2
  522.5 1.2 subtract_convert_fusion
  523.7 0.1 copy.83
  523.8 4.1 convolution_convert_fusion
  527.9 0.9 copy-done.4
  528.8 0.2 fusion.4
  529.1 0.1 copy.74
  529.2 0.7 convert_element_type.95
  529.9 105.5 %reduce-scatter.8.cloned.1.call-done = bf16[320,16]{0,1:T(8,128)(2,1)} async-done(((bf16[320,512]{0,1:T(8,128)(2,1)}), bf16[320,16]{0,1:T(8,128)(2,1)}) %reduce-scatter.8.cloned.1.call-update) | async-done | bytes 10256 | tf_op jit(solution)/shard_map/reduce_scatter | solution.py:137
  635.4 1.3 convert_element_type.108
  636.8 105.7 %reduce-scatter.6.cloned.1.call-done = bf16[320,16]{0,1:T(8,128)(2,1)} async-done(((bf16[320,512]{0,1:T(8,128)(2,1)}), bf16[320,16]{0,1:T(8,128)(2,1)}) %reduce-scatter.6.cloned.1.call-update) | async-done | bytes 10256 | tf_op jit(solution)/shard_map/reduce_scatter | solution.py:134
  742.5 1.3 convert_element_type.105
  743.8 123.4 %reduce-scatter.4.cloned.1.call-done = bf16[160,256]{1,0:T(8,128)(2,1)} async-done(((bf16[5120,256]{1,0:T(8,128)(2,1)}), bf16[160,256]{1,0:T(8,128)(2,1)}) %reduce-scatter.4.cloned.1.call-update) | async-done | bytes 81936 | tf_op jit(solution)/shard_map/reduce_scatter | solution.py:131
  867.2 1.6 convert_element_type.102
  (64 shorter events, 0.8 us)
Async XLA Ops:
  7.2 324.8 %copy-start = (bf16[5120,256]{1,0:T(8,128)(2,1)S(1)}, bf16[5120,256]{1,0:T(8,128)(2,1)}, u32[]{:S(2)}) copy-start(bf16[5120,256]{1,0:T(8,128)(2,1)} %param.17) | copy-start | bytes 7864324
  7.2 23.6 %copy-start.14 = (s32[8]{0:T(128)S(1)}, s32[8]{0:T(128)}, u32[]{:S(2)}) copy-start(s32[8]{0:T(128)} %param.13) | copy-start | bytes 100
  11.4 63.6 %copy-start.15 = (f32[8]{0:T(128)S(1)}, f32[8]{0:T(128)}, u32[]{:S(2)}) copy-start(f32[8]{0:T(128)} %param.15) | copy-start | bytes 100
  11.4 63.6 %copy-start.16 = (s32[8]{0:T(128)S(1)}, s32[8]{0:T(128)}, u32[]{:S(2)}) copy-start(s32[8]{0:T(128)} %param.14) | copy-start | bytes 100
  11.4 58.2 %all-to-all-start = ((bf16[32,32,320]{2,1,0:T(8,128)(2,1)}), bf16[32,32,320]{2,1,0:T(8,128)(2,1)S(1)}, u32[]{:S(2)}, u32[]{:S(2)}) async-start(bf16[32,32,320]{2,1,0:T(8,128)(2,1)} %select_select_fusion), calls=%async_computation | async-start | bytes 1572864 | tf_op jit(solution)/shard_map/all_to_all | solution.py:90
  30.8 203.6 %all-reduce.5.cloned.1.call-start = ((), (), s32[]{:S(2)}) async-start(), calls=%async_computation.4 | async-start | bytes 1048576 | tf_op jit(solution)/shard_map/psum | solution.py:99
  74.0 258.0 %all-gather.2.cloned.1.call-start = ((), (), s32[]{:S(2)}) async-start(), calls=%async_computation.5 | async-start | bytes 2785280 | tf_op jit(solution)/shard_map/all_gather | solution.py:93
  74.9 440.9 %all-reduce.7.cloned.1.call-start = ((), (), s32[]{:S(2)}) async-start(), calls=%async_computation.9 | async-start | bytes 1048576 | tf_op jit(solution)/shard_map/psum | solution.py:122
  75.0 265.6 %copy-start.17 = (f32[8]{0:T(128)}, f32[8]{0:T(128)S(1)}, u32[]{:S(2)}) copy-start(f32[8]{0:T(128)S(1)} %multiply_multiply_fusion.2) | copy-start | bytes 100
  235.5 104.7 %copy-start.9 = (f32[128]{0:T(128)S(1)}, f32[128]{0:T(128)}, u32[]{:S(2)}) copy-start(f32[128]{0:T(128)} %param.20) | copy-start | bytes 1540
  235.5 104.7 %copy-start.11 = (f32[128]{0:T(128)S(1)}, f32[128]{0:T(128)}, u32[]{:S(2)}) copy-start(f32[128]{0:T(128)} %param.21) | copy-start | bytes 1540
  337.5 6.3 copy-start.1
  339.5 3.2 copy-start.13
  339.5 4.4 copy-start.10
  339.5 4.4 copy-start.12
  340.6 5.5 copy-start.3
  340.6 5.5 copy-start.5
  340.7 6.1 copy-start.7
  342.7 1.0 copy-start.2
  346.8 288.7 %reduce-scatter.8.cloned.1.call-start = ((), (), s32[]{:S(2)}) async-start(), calls=%async_computation.8 | async-start | bytes 405504 | tf_op jit(solution)/shard_map/reduce_scatter | solution.py:137
  517.9 224.6 %reduce-scatter.6.cloned.1.call-start = ((), (), s32[]{:S(2)}) async-start(), calls=%async_computation.7 | async-start | bytes 405504 | tf_op jit(solution)/shard_map/reduce_scatter | solution.py:134
  522.4 344.8 %reduce-scatter.4.cloned.1.call-start = ((), (), s32[]{:S(2)}) async-start(), calls=%async_computation.6 | async-start | bytes 2703360 | tf_op jit(solution)/shard_map/reduce_scatter | solution.py:131
  527.9 0.9 copy-start.4
  527.9 1.0 copy-start.6
  527.9 1.0 copy-start.8
Sparse Core Ops, SparseCore 0:
  74.1 160.1 all-reduce.4
  237.2 94.7 all-gather.1
  346.9 168.8 all-reduce.6
  520.0 115.3 reduce-scatter.7
  639.6 102.7 reduce-scatter.5
  746.8 120.3 reduce-scatter.3
where the time goes:
time: 878 us; the launch traced here: 876 us
  waiting for transfers between devices  711 us (81%)
  blocking collectives  85.9 us (10%)
  matrix products  20.6 us (2%)
  starting transfers between devices  19.6 us (2%)
  between operations  14.5 us (2%)
  local copies, waits for them, and re-layouts  12 us (1%)
  other arithmetic  12 us (1%)
    psum x1, waiting for transfers between devices, local(): lax.psum(key_place.astype(jnp.bfloat16), 'mp').astype(jnp.float32)  169 us
    reduce_scatter x1, waiting for transfers between devices, local(): lax.psum_scatter(query_whole.astype(jnp.bfloat16), 'dp', scatter_dimensio...  123 us
    reduce_scatter x1, waiting for transfers between devices, local(): lax.psum_scatter(key_term.astype(jnp.bfloat16), 'dp', scatter_dimension=1...  106 us
    reduce_scatter x1, waiting for transfers between devices, local(): lax.psum_scatter(value_term.astype(jnp.bfloat16), 'dp', scatter_dimension...  105 us
    all_gather x1, waiting for transfers between devices, local(): piece = lax.all_gather(local_rows, 'mp', axis=1, tiled=True)  96.5 us
    psum x1, blocking collectives, local(): key_all, value_all = lax.psum((key_part, value_part), 'mp')  85.9 us
    psum x1, waiting for transfers between devices, local(): key_all, value_all = lax.psum((key_part, value_part), 'mp')  72.2 us
    all_to_all x1, waiting for transfers between devices, local(): lax.all_to_all(outgoing, 'dp', split_axis=0, concat_axis=0, tiled=True)  38.6 us
  transfers between devices with their start and end apart: 7, of which 7 were waited for; matrix products, arithmetic and copies ran while one was open for 2% of the time, Pallas kernels for 0%

commit v1 on v0

v1 whole, which is shorter than its diff:
```python
import functools
import math

import jax
import jax.numpy as jnp
from jax import lax
from jax.experimental import pallas as pl
from jax.experimental.pallas import tpu as pltpu
from jax.sharding import PartitionSpec as P

F32, BF16 = jnp.float32, jnp.bfloat16
MESH = pl.DeviceIdType.MESH

N_X, N_ZH, N_CORE, N_Y, N_ZL = 4, 4, 2, 4, 4
N_DP, N_MP = N_X * N_ZH * N_CORE, N_Y * N_ZL
SEQS, LENGTH, WIDTH = 8, 32, 320
TOKENS = SEQS * LENGTH
HEAD, COLS = 128, 256
PADDED = 384
SHARE = WIDTH // N_X
HALF = WIDTH // 2
EPS = 1e-6
SCALE = 1.0 / math.sqrt(HEAD)


def dot_nn(a, b):
    return lax.dot_general(a, b, (((1,), (0,)), ((), ())), preferred_element_type=F32)


def dot_tn(a, b):
    return lax.dot_general(a, b, (((0,), (0,)), ((), ())), preferred_element_type=F32)


def dot_nt(a, b):
    return lax.dot_general(a, b, (((1,), (1,)), ((), ())), preferred_element_type=F32)


def rms_back(values, inverse, gain, grad_out):
    scaled = grad_out * gain
    inner = jnp.mean(values * scaled, axis=0, keepdims=True)
    return inverse * scaled - values * (inverse * inverse * inverse) * inner


def kernel(
    table,
    source,
    x_ref,
    w_mine,
    w_query,
    d_out,
    target,
    q_gain,
    k_gain,
    att_out,
    gq_out,
    gkv_out,
    piece,
    w_kv,
    d_send,
    d_slots,
    acc_q,
    acc_kv,
    att,
    att_send,
    att_slots,
    d_query,
    g_send,
    g_recv,
    g_keep,
    x_recv,
    z_send,
    z_recv,
    dkv,
    dkv_recv,
    dkv_all,
    kv_part,
    kv_recv,
    kv_sum,
    kv_x,
    kv_zs,
    kv_z,
    tz_s,
    tz_r,
    ty_s,
    ty_r,
    tf_s,
    tf_r,
    w1_s,
    w1_r,
    w2_s,
    w2_r,
    w3_s,
    w3_r,
    co_s,
    co_r,
    at_s,
    at_r,
    k1_s,
    k1_r,
    k2_s,
    k2_r,
    k3_s,
    k3_r,
    gc_s,
    gc_r,
    gx_s,
    gx_r,
    gz_s,
    gz_r,
    vc_s,
    vc_r,
    vx_s,
    vx_r,
    vz_s,
    vz_r,
):
    dp, mp = lax.axis_index("dp"), lax.axis_index("mp")
    x, zh, core = dp // (N_ZH * N_CORE), (dp // N_CORE) % N_ZH, dp % N_CORE
    y, zl = mp // N_ZL, mp % N_ZL
    other = 1 - core

    def at_dp(step):
        return lax.rem(dp + step, N_DP), mp

    def at_mp(step):
        return dp, lax.rem(mp + step, N_MP)

    def at_x(step):
        return lax.rem(dp + step * (N_ZH * N_CORE), N_DP), mp

    def at_zh(step):
        return x * (N_ZH * N_CORE) + lax.rem(zh + step, N_ZH) * N_CORE + core, mp

    def at_y(step):
        return dp, lax.rem(mp + step * N_ZL, N_MP)

    def at_zl(step):
        return dp, y * N_ZL + lax.rem(zl + step, N_ZL)

    sibling = (dp + 1 - 2 * core, mp)

    def copy(src, dst, send, recv, device):
        return pltpu.make_async_remote_copy(
            src_ref=src,
            dst_ref=dst,
            send_sem=send,
            recv_sem=recv,
            device_id=device,
            device_id_type=MESH,
        )

    sends = []

    def start(*args):
        made = copy(*args)
        made.start()
        sends.append(made)

    barrier = pltpu.get_barrier_semaphore()
    for step in range(1, N_DP):
        pl.semaphore_signal(barrier, inc=1, device_id=at_dp(step), device_id_type=MESH)
    for step in range(1, N_MP):
        pl.semaphore_signal(barrier, inc=1, device_id=at_mp(step), device_id_type=MESH)
    pl.semaphore_wait(barrier, N_DP - 1 + N_MP - 1)

    def block(step_y, step_z):
        return lax.rem(y + step_y, N_Y) * N_ZL + lax.rem(zl + step_z, N_ZL)

    def mine(step):
        return block(0, N_ZL - step)

    def near(k, way):
        return block(N_Y - 1 if way == 0 else 1, N_ZL - k if k else 0)

    piece[mp] = x_ref[:WIDTH]
    tokens = x_ref.at[pl.ds(0, WIDTH)]
    for k in (1, 2, 3):
        start(tokens, piece.at[mp], tz_s.at[k], tz_r.at[k], at_zl(k))
    for way, step in ((0, 1), (1, N_Y - 1)):
        start(tokens, piece.at[mp], ty_s.at[0, way], ty_r.at[0, way], at_y(step))

    rows = pl.ds(pl.multiple_of(x * SHARE, 16), SHARE)
    w_kv[core, mp, rows] = w_mine[y]
    for step in range(1, N_MP):
        dest = at_mp(step)
        start(w_mine.at[dest[1] // N_ZL], w_kv.at[core, mp, rows], w1_s, w1_r, dest)

    for k in range(N_DP):
        wanted = lax.rem(dp + k, N_DP)
        slot = jnp.int32(SEQS)
        for s in range(SEQS):
            slot = jnp.where(source[s] == wanted, jnp.int32(s), slot)
        d_send[k] = d_out[slot]
        if k:
            start(d_send.at[k], d_slots.at[k], co_s, co_r, at_dp(k))
    d_slots[0] = d_send[0]

    acc_q[...] = jnp.zeros_like(acc_q)

    def project(j):
        place = pl.ds(pl.multiple_of(j * WIDTH, WIDTH), WIDTH)
        acc_q[...] += dot_tn(w_query[place], piece[j])

    def wait_near(k, way):
        spot = piece.at[near(k, way)]
        copy(spot, spot, ty_s.at[k, way], ty_r.at[k, way], at_y(1)).wait_recv()

    def pass_on(k):
        for way, step in ((0, 1), (1, N_Y - 1)):
            wait_near(k, way)
            half = piece.at[near(k, way), pl.ds(way * HALF, HALF)]
            start(half, half, tf_s.at[k, way], tf_r.at[k, way], at_y(step))

    def take(k):
        spot = piece.at[mine(k)]
        copy(spot, spot, tz_s.at[k], tz_r.at[k], at_zl(1)).wait_recv()
        for way, step in ((0, 1), (1, N_Y - 1)):
            start(spot, spot, ty_s.at[k, way], ty_r.at[k, way], at_y(step))

    project(mp)
    take(1)
    project(mine(1))
    pass_on(0)
    take(2)
    project(mine(2))
    take(3)
    project(mine(3))
    got = w_kv.at[0, pl.ds(0, N_MP - 1), pl.ds(0, SHARE)]
    copy(got, got, w1_s, w1_r, at_mp(1)).wait_recv()
    part = w_kv.at[core, :, rows]
    for k in (1, 2, 3):
        start(part, part, w2_s.at[k], w2_r.at[k], at_x(k))
    for way in (0, 1):
        project(near(0, way))
    for k in (1, 2, 3):
        pass_on(k)
        for way in (0, 1):
            project(near(k, way))
    for k in (1, 2, 3):
        copy(part, part, w2_s.at[k], w2_r.at[k], at_x(k)).wait_recv()
    start(w_kv.at[core], w_kv.at[core], w3_s, w3_r, sibling)
    for k in range(N_ZL):
        far = block(2, N_ZL - k if k else 0)
        for way in (0, 1):
            half = piece.at[far, pl.ds(way * HALF, HALF)]
            copy(half, half, tf_s.at[k, way], tf_r.at[k, way], at_y(1)).wait_recv()
        project(far)
    copy(w_kv.at[other], w_kv.at[other], w3_s, w3_r, sibling).wait_recv()
    acc_kv[...] = jnp.zeros_like(acc_kv)

    def project_kv(j, carry):
        for half in (0, 1):
            acc_kv[half] += dot_tn(w_kv[half, j], piece[j])
        return carry

    lax.fori_loop(0, N_MP, project_kv, 0)

    gain_q, gain_k = q_gain[...], k_gain[...]
    key_sum = acc_kv[0]
    k_inverse = lax.rsqrt(jnp.mean(key_sum * key_sum, axis=0, keepdims=True) + EPS)
    k_norm = (key_sum * k_inverse * gain_k).astype(BF16)
    value = acc_kv[1].astype(BF16)
    at_key = lax.broadcasted_iota(jnp.int32, (TOKENS, TOKENS), 0)
    at_query = lax.broadcasted_iota(jnp.int32, (TOKENS, TOKENS), 1)
    seen = ((at_key >> 5) == (at_query >> 5)) & (at_key <= at_query)
    saved = []
    for h in range(COLS // HEAD):
        query = acc_q[h * HEAD : (h + 1) * HEAD]
        inverse = lax.rsqrt(jnp.mean(query * query, axis=0, keepdims=True) + EPS)
        q_norm = (query * inverse * gain_q).astype(BF16)
        scores = jnp.where(seen, dot_tn(k_norm, q_norm) * SCALE, -1e30)
        raised = jnp.exp(scores - jnp.max(scores, axis=0, keepdims=True))
        probs = raised / jnp.sum(raised, axis=0, keepdims=True)
        p_half = probs.astype(BF16)
        out = dot_nn(value, p_half).T.astype(BF16)
        att[:, :, h * HEAD : (h + 1) * HEAD] = out.reshape(SEQS, LENGTH, HEAD)
        saved.append((query, inverse, q_norm, probs, p_half))
    for k in range(N_DP):
        spot = table[0, lax.rem(dp + k, N_DP)]
        att_send[k] = att[jnp.maximum(spot, 0)]
        if k:
            start(att_send.at[k], att_slots.at[k], at_s, at_r, at_dp(k))
    att_slots[0] = att_send[0]

    got = d_slots.at[pl.ds(1, N_DP - 1)]
    copy(got, got, co_s, co_r, at_dp(1)).wait_recv()
    place = lax.broadcasted_iota(jnp.int32, (TOKENS, N_DP * LENGTH), 0)
    chosen = jnp.where(place == target[...], 1.0, 0.0).astype(BF16)
    d_rows = dot_nn(chosen, d_slots[...].reshape(N_DP * LENGTH, COLS))
    d_cols = d_rows.T.astype(BF16)
    d_knorm = jnp.zeros((HEAD, TOKENS), F32)
    d_value = jnp.zeros((HEAD, TOKENS), F32)
    d_queries = []
    for h in range(COLS // HEAD):
        query, inverse, q_norm, probs, p_half = saved[h]
        out_half = d_cols[h * HEAD : (h + 1) * HEAD]
        d_probs = dot_tn(value, out_half)
        d_value += dot_nt(out_half, p_half)
        centred = d_probs - jnp.sum(d_probs * probs, axis=0, keepdims=True)
        score_half = (probs * centred * SCALE).astype(BF16)
        d_qnorm = dot_nn(k_norm, score_half)
        d_knorm += dot_nt(q_norm, score_half)
        d_queries.append(rms_back(query, inverse, gain_q, d_qnorm))
    for h in range(COLS // HEAD):
        d_query[:, h * HEAD : (h + 1) * HEAD] = d_queries[h].T.astype(BF16)
    d_key = rms_back(key_sum, k_inverse, gain_k, d_knorm).astype(BF16)
    d_value = d_value.astype(BF16)
    for q in (0, 1):
        dkv[q] = d_key[q * 64 : (q + 1) * 64]
        dkv[2 + q] = d_value[q * 64 : (q + 1) * 64]

    for k in (1, 2, 3):
        start(
            dkv.at[lax.rem(zl + k, N_ZL)],
            dkv_recv.at[k],
            k1_s.at[k],
            k1_r.at[k],
            at_zl(k),
        )

    def partial_rows(to, into, which):
        def one(i, carry):
            rows = pl.ds(pl.multiple_of(which * HALF, 16), HALF)
            total = dot_nn(piece[to * N_ZH + i, rows], d_query[...])
            into[to, i] = total.astype(BF16)
            return carry

        lax.fori_loop(0, N_ZH, one, 0)

    def x_at(step):
        return lax.rem(x + step, N_X)

    order = (2, 1, 3, 0)
    for k in order:
        to = x_at(k)
        partial_rows(to, g_send, other)
        start(g_send.at[to], g_recv.at[to], gc_s.at[k], gc_r.at[k], sibling)
    for k in order:
        partial_rows(x_at(k), g_keep, core)

    for k in (1, 2, 3):
        copy(
            dkv.at[0], dkv_recv.at[k], k1_s.at[k], k1_r.at[k], at_zl(k)
        ).wait_recv()
    total = dkv[zl].astype(F32)
    for k in (1, 2, 3):
        total += dkv_recv[k].astype(F32)
    dkv_all[y, zl] = total.astype(BF16)
    spot = dkv_all.at[y, zl]
    for k in (1, 2, 3):
        start(spot, spot, k2_s.at[k], k2_r.at[k], at_zl(k))

    for k in order:
        to = x_at(k)
        copy(
            g_send.at[to], g_recv.at[to], gc_s.at[k], gc_r.at[k], sibling
        ).wait_recv()
        both = g_keep[to].astype(F32) + g_recv[to].astype(F32)
        g_keep[to] = both.astype(BF16)
        if k:
            for kz in order:
                to_z = lax.rem(zh + kz, N_ZH)
                start(
                    g_keep.at[to, to_z],
                    x_recv.at[k, to_z],
                    gx_s.at[k, kz],
                    gx_r.at[k, kz],
                    at_x(k),
                )

    for k in (1, 2, 3):
        copy(spot, spot, k2_s.at[k], k2_r.at[k], at_zl(k)).wait_recv()
    group = dkv_all.at[y]
    for k in (1, 2, 3):
        start(group, group, k3_s.at[k], k3_r.at[k], at_y(k))
    for k in (1, 2, 3):
        copy(group, group, k3_s.at[k], k3_r.at[k], at_y(k)).wait_recv()

    def kv_rows(g, carry):
        rows = dkv_all[g].reshape(2 * HEAD, TOKENS)
        product = dot_nt(rows, x_ref[...]).astype(BF16)
        for half in range(2):
            for i in range(N_ZH):
                for c in range(N_CORE):
                    first = half * HEAD + i * 32 + c * 16
                    kv_part[c, g, i, half] = product[first : first + 16]
        return carry

    lax.fori_loop(0, N_X, kv_rows, 0)
    start(kv_part.at[other], kv_recv, vc_s, vc_r, sibling)

    for kz in order:
        to_z = lax.rem(zh + kz, N_ZH)
        total = g_keep[x, to_z].astype(F32)
        for k in (1, 2, 3):
            spot = x_recv.at[k, to_z]
            copy(spot, spot, gx_s.at[k, kz], gx_r.at[k, kz], at_x(k)).wait_recv()
            total += x_recv[k, to_z].astype(F32)
        z_send[to_z] = total.astype(BF16)
        if kz:
            start(
                z_send.at[to_z], z_recv.at[kz], gz_s.at[kz], gz_r.at[kz], at_zh(kz)
            )

    copy(kv_part.at[other], kv_recv, vc_s, vc_r, sibling).wait_recv()
    kv_sum[...] = (kv_part[core].astype(F32) + kv_recv[...].astype(F32)).astype(BF16)
    for k in (1, 2, 3):
        start(kv_sum.at[x_at(k)], kv_x.at[k], vx_s.at[k], vx_r.at[k], at_x(k))
    total = kv_sum[x].astype(F32)
    for k in (1, 2, 3):
        copy(kv_sum.at[0], kv_x.at[k], vx_s.at[k], vx_r.at[k], at_x(k)).wait_recv()
        total += kv_x[k].astype(F32)
    kv_zs[...] = total.astype(BF16)
    for k in (1, 2, 3):
        to_z = lax.rem(zh + k, N_ZH)
        start(kv_zs.at[to_z], kv_z.at[k], vz_s.at[k], vz_r.at[k], at_zh(k))

    total = z_send[zh].astype(F32)
    for k in (1, 2, 3):
        copy(z_send.at[0], z_recv.at[k], gz_s.at[k], gz_r.at[k], at_zh(k)).wait_recv()
        total += z_recv[k].astype(F32)
    gq_out[...] = total

    total = kv_zs[zh].astype(F32)
    for k in (1, 2, 3):
        copy(kv_zs.at[0], kv_z.at[k], vz_s.at[k], vz_r.at[k], at_zh(k)).wait_recv()
        total += kv_z[k].astype(F32)
    gkv_out[...] = total

    got = att_slots.at[pl.ds(1, N_DP - 1)]
    copy(got, got, at_s, at_r, at_dp(1)).wait_recv()
    for s in range(SEQS):
        att_out[s] = att_slots[lax.rem(dp + N_DP - source[s], N_DP)]

    for made in sends:
        made.wait_send()


def local(
    pool,
    send_table,
    slot_source,
    multiplicity,
    slot_weight,
    cotangent,
    w_query,
    w_key,
    w_value,
    query_gain,
    key_gain,
):
    dp = lax.axis_index("dp")
    rank_x, core = dp // (N_ZH * N_CORE), dp % N_CORE
    rows = pool.reshape(TOKENS, WIDTH).T
    rows = jnp.pad(rows, ((0, PADDED - WIDTH), (0, 0)))
    weights = jnp.where(core == 0, w_key, w_value)
    weights = lax.dynamic_slice_in_dim(weights, rank_x * SHARE, SHARE, 0)
    weights = weights.reshape(SHARE, N_Y, HEAD).transpose(1, 0, 2)
    factor = multiplicity.astype(F32) * slot_weight / LENGTH
    d_out = (cotangent.astype(F32) * factor[:, None, None]).astype(BF16)
    d_out = jnp.pad(d_out, ((0, 1), (0, 0), (0, 0)))
    entry = send_table[0, (dp + N_DP - jnp.arange(N_DP)) % N_DP]
    target = jnp.where(
        entry[:, None] >= 0, entry[:, None] * LENGTH + jnp.arange(LENGTH)[None, :], -1
    ).reshape(1, N_DP * LENGTH)

    dma = pltpu.SemaphoreType.DMA
    smem = pl.BlockSpec(memory_space=pltpu.SMEM)
    vmem = pl.BlockSpec(memory_space=pltpu.VMEM)
    attended, grad_query, grad_kv = pl.pallas_call(
        kernel,
        out_shape=(
            jax.ShapeDtypeStruct((SEQS, LENGTH, COLS), BF16),
            jax.ShapeDtypeStruct((HALF, COLS), F32),
            jax.ShapeDtypeStruct((2, 16, PADDED), F32),
        ),
        in_specs=[smem, smem] + [vmem] * 7,
        out_specs=(vmem, vmem, vmem),
        scratch_shapes=[
            pltpu.VMEM((N_MP, WIDTH, TOKENS), BF16),
            pltpu.VMEM((2, N_MP, WIDTH, HEAD), BF16),
            pltpu.VMEM((N_DP, LENGTH, COLS), BF16),
            pltpu.VMEM((N_DP, LENGTH, COLS), BF16),
            pltpu.VMEM((COLS, TOKENS), F32),
            pltpu.VMEM((2, HEAD, TOKENS), F32),
            pltpu.VMEM((SEQS, LENGTH, COLS), BF16),
            pltpu.VMEM((N_DP, LENGTH, COLS), BF16),
            pltpu.VMEM((N_DP, LENGTH, COLS), BF16),
            pltpu.VMEM((TOKENS, COLS), BF16),
            pltpu.VMEM((N_X, N_ZH, HALF, COLS), BF16),
            pltpu.VMEM((N_X, N_ZH, HALF, COLS), BF16),
            pltpu.VMEM((N_X, N_ZH, HALF, COLS), BF16),
            pltpu.VMEM((N_X, N_ZH, HALF, COLS), BF16),
            pltpu.VMEM((N_ZH, HALF, COLS), BF16),
            pltpu.VMEM((N_ZH, HALF, COLS), BF16),
            pltpu.VMEM((N_ZL, 64, TOKENS), BF16),
            pltpu.VMEM((N_ZL, 64, TOKENS), BF16),
            pltpu.VMEM((N_Y, N_ZL, 64, TOKENS), BF16),
            pltpu.VMEM((N_CORE, N_X, N_ZH, 2, 16, PADDED), BF16),
            pltpu.VMEM((N_X, N_ZH, 2, 16, PADDED), BF16),
            pltpu.VMEM((N_X, N_ZH, 2, 16, PADDED), BF16),
            pltpu.VMEM((N_X, N_ZH, 2, 16, PADDED), BF16),
            pltpu.VMEM((N_ZH, 2, 16, PADDED), BF16),
            pltpu.VMEM((N_ZH, 2, 16, PADDED), BF16),
            dma((4,)),
            dma((4,)),
            dma((4, 2)),
            dma((4, 2)),
            dma((4, 2)),
            dma((4, 2)),
            dma,
            dma,
            dma((4,)),
            dma((4,)),
            dma,
            dma,
            dma,
            dma,
            dma,
            dma,
            dma((4,)),
            dma((4,)),
            dma((4,)),
            dma((4,)),
            dma((4,)),
            dma((4,)),
            dma((4,)),
            dma((4,)),
            dma((4, 4)),
            dma((4, 4)),
            dma((4,)),
            dma((4,)),
            dma,
            dma,
            dma((4,)),
            dma((4,)),
            dma((4,)),
            dma((4,)),
        ],
        compiler_params=pltpu.CompilerParams(
            collective_id=0, has_side_effects=True, vmem_limit_bytes=48 * 1024 * 1024
        ),
        name="train_step",
    )(
        send_table,
        slot_source,
        rows,
        weights,
        w_query,
        d_out,
        target,
        query_gain[:, None],
        key_gain[:, None],
    )
    key_gradient, grad_value = grad_kv[0, :, :WIDTH].T, grad_kv[1, :, :WIDTH].T
    return attended, grad_query, key_gradient, grad_value


def solution(mesh):
    return jax.shard_map(
        local,
        mesh=mesh,
        in_specs=(
            P("dp", None, "mp"),
            P("dp", None),
            P("dp"),
            P("dp"),
            P("dp"),
            P("dp", None, "mp"),
            P(None, "mp"),
            P("mp", None),
            P("mp", None),
            P(),
            P(),
        ),
        out_specs=(P("dp", None, "mp"), P("dp", "mp"), P("mp", "dp"), P("mp", "dp")),
        check_vma=False,
    )
```

time: 878 us -> 162 us (0.18)
  waiting for transfers between devices: 711 us -> 0 us
  Pallas kernels: 0 us -> 149 us
  blocking collectives: 85.9 us -> 0 us
  matrix products: 20.6 us -> 0 us
  starting transfers between devices: 19.6 us -> 0 us
  between operations: 14.5 us -> 0.72 us
  other arithmetic: 12 us -> 2.73 us
    reduce_scatter x3 -> x0, waiting for transfers between devices: 335 us -> none  [the longest x1 123 us: local(): lax.psum_scatter(query_whole.astype(jnp.bfloat16), 'dp', scatter_dimensio...]
    psum x2 -> x0, waiting for transfers between devices: 241 us -> none  [the longest x1 169 us: local(): lax.psum(key_place.astype(jnp.bfloat16), 'mp').astype(jnp.float32)]
    pallas_call x0 -> x1, Pallas kernels: none -> 149 us  [local(): pl.pallas_call(kernel, out_shape=(jax.ShapeDtypeStruct((SEQS, LENGTH, COL...]
    all_gather x1 -> x0, waiting for transfers between devices: 96.5 us -> none  [local(): piece = lax.all_gather(local_rows, 'mp', axis=1, tiled=True)]
    psum x1 -> x0, blocking collectives: 85.9 us -> none  [local(): key_all, value_all = lax.psum((key_part, value_part), 'mp')]
    all_to_all x1 -> x0, waiting for transfers between devices: 38.6 us -> none  [local(): lax.all_to_all(outgoing, 'dp', split_axis=0, concat_axis=0, tiled=True)]
    dot_general x12 -> x0, matrix products: 20.6 us -> none  [the longest x1 4.08 us: local(): jnp.einsum('td,tc->dc', piece, query_rows, preferred_element_type=jnp.flo...]
    all_to_all x1 -> x0, starting transfers between devices: 19.3 us -> none  [local(): lax.all_to_all(outgoing, 'dp', split_axis=0, concat_axis=0, tiled=True)]
  transfers between devices with their start and end apart: 7 -> 0, of which waited for: 7 -> 0; matrix products, arithmetic and copies ran while one was open for 2% -> 0% of each run, Pallas kernels for 0% -> 0%
where the time goes in v1:
time: 162 us; the launch traced here: 161 us
  Pallas kernels  149 us (92%)
  local copies, waits for them, and re-layouts  9.01 us (6%)
  other arithmetic  2.73 us (2%)
    pallas_call x1, Pallas kernels, local(): pl.pallas_call(kernel, out_shape=(jax.ShapeDtypeStruct((SEQS, LENGTH, COL...  149 us
    unnamed x8, local copies, waits for them, and re-layouts  4.37 us

profile of v1, /device:TPU:1, one launch (start us, length us, event | category | flops | bytes accessed | tf_op | source)
XLA Modules:
  0.0 161.2 jit_solution(10439617483399881357)
XLA Ops:
  0.7 1.3 gather_fusion
  2.0 0.7 multiply_multiply_fusion
  2.7 0.1 add_select_fusion
  2.8 0.1 select_n.67.target
  2.9 0.8 copy.20.q_gain
  3.7 0.8 copy.21.k_gain
  4.4 1.0 bitcast_bitcast_fusion.w_mine
  5.4 1.0 multiply_convert_fusion
  6.4 1.0 copy.18
  7.5 0.0 copy-start
  7.5 0.6 copy-done
  8.1 0.0 copy-start.1
  8.1 1.7 %copy-done.1 = bf16[5120,256]{1,0:T(8,128)(2,1)S(1)} copy-done((bf16[5120,256]{1,0:T(8,128)(2,1)S(1)}, bf16[5120,256]{1,0:T(8,128)(2,1)}, u32[]{:S(2)}) %copy-start.1) | copy-done | bytes 2621464
  9.9 0.0 copy-start.2
  9.9 0.7 copy-done.2
  10.5 148.8 %train_step.1 = (bf16[8,32,256]{2,1,0:T(8,128)(2,1)S(1)}, f32[160,256]{1,0:T(8,128)S(1)}, f32[2,16,384]{2,1,0:T(8,128)S(1)}) custom-call(s32[1,32]{1,0:T(1,128)S(1)} %copy-done, s32[8]{0:T(128)S(1)} %copy-done.2, bf16[384,256]{1,0:T(8,128)(2,1)S(1)} %pad.9.x_ref, bf16[4,80,128]{2,1,0:T(8,128)(2,1)S(1)} %bitcast_bitcast_fusion.w_mine, ...), custom_call_target="tpu_custom_call" | custom-call | tf_op jit(solution)/shard_map/train_step/pallas_call | solution.py:470
  159.3 0.6 slice_bitcast_fusion
  159.9 0.7 copy.26
  160.6 0.7 copy.27
  (5 shorter events, 0.1 us)
Async XLA Ops:
  7.5 0.7 copy-start
  8.1 1.7 %copy-start.1 = (bf16[5120,256]{1,0:T(8,128)(2,1)S(1)}, bf16[5120,256]{1,0:T(8,128)(2,1)}, u32[]{:S(2)}) copy-start(bf16[5120,256]{1,0:T(8,128)(2,1)} %w_query.1) | copy-start | bytes 7864324
  9.9 0.7 copy-start.2

commit v2 on v1

--- a/solution.py
+++ b/solution.py
@@ -20,6 +20,7 @@
 SHARE = WIDTH // N_X
 HALF = WIDTH // 2
 EPS = 1e-6
+PAIRS = ((0, 1), (1, 0), (1, 1), (2, 0), (2, 1), (3, 0), (3, 1))
 SCALE = 1.0 / math.sqrt(HEAD)
 
 
@@ -42,25 +43,57 @@
 
 
 def kernel(
+    table_in,
+    source_in,
+    drawn_in,
+    weight_in,
+    pool_in,
+    cotangent_in,
+    w_query_in,
+    w_key_in,
+    w_value_in,
+    q_gain_in,
+    k_gain_in,
+    att_out,
+    gq_out,
+    gk_out,
+    gv_out,
     table,
     source,
+    drawn,
+    weight,
+    pool,
+    cotangent,
+    w_query,
+    w_key,
+    w_value,
+    q_gain,
+    k_gain,
+    load_s,
+    table_row,
+    source_row,
+    tables,
+    sources,
+    near_tables,
+    near_sources,
+    ts_s,
+    ts_r,
     x_ref,
     w_mine,
-    w_query,
-    d_out,
-    target,
-    q_gain,
-    k_gain,
-    att_out,
-    gq_out,
-    gkv_out,
     piece,
     w_kv,
+    d_all_0,
+    d_all_1,
+    d_all_2,
+    d_all_3,
     d_send,
     d_slots,
     acc_q,
     acc_kv,
-    att,
+    att_all_0,
+    att_all_1,
+    att_all_2,
+    att_all_3,
     att_send,
     att_slots,
     d_query,
@@ -91,10 +124,18 @@
     w2_r,
     w3_s,
     w3_r,
-    co_s,
-    co_r,
-    at_s,
-    at_r,
+    c1_s,
+    c1_r,
+    cf_s,
+    cf_r,
+    c2_s,
+    c2_r,
+    a1_s,
+    a1_r,
+    af_s,
+    af_r,
+    a2_s,
+    a2_r,
     k1_s,
     k1_r,
     k2_s,
@@ -119,8 +160,10 @@
     y, zl = mp // N_ZL, mp % N_ZL
     other = 1 - core
 
-    def at_dp(step):
-        return lax.rem(dp + step, N_DP), mp
+    def pair(step, flip):
+        return lax.rem(x + step, N_X) * (N_ZH * N_CORE) + zh * N_CORE + (
+            other if flip else core
+        )
 
     def at_mp(step):
         return dp, lax.rem(mp + step, N_MP)
@@ -138,6 +181,8 @@
         return dp, y * N_ZL + lax.rem(zl + step, N_ZL)
 
     sibling = (dp + 1 - 2 * core, mp)
+    d_all = (d_all_0, d_all_1, d_all_2, d_all_3)
+    att_all = (att_all_0, att_all_1, att_all_2, att_all_3)
 
     def copy(src, dst, send, recv, device):
         return pltpu.make_async_remote_copy(
@@ -157,11 +202,50 @@
         sends.append(made)
 
     barrier = pltpu.get_barrier_semaphore()
-    for step in range(1, N_DP):
-        pl.semaphore_signal(barrier, inc=1, device_id=at_dp(step), device_id_type=MESH)
-    for step in range(1, N_MP):
-        pl.semaphore_signal(barrier, inc=1, device_id=at_mp(step), device_id_type=MESH)
-    pl.semaphore_wait(barrier, N_DP - 1 + N_MP - 1)
+    partners = [at_mp(step) for step in range(1, N_MP)]
+    partners += [at_zh(step) for step in range(1, N_ZH)]
+    partners += [(pair(step, flip), mp) for step, flip in PAIRS]
+    for device in partners:
+        pl.semaphore_signal(barrier, inc=1, device_id=device, device_id_type=MESH)
+
+    loads = {}
+    for i, (name, src, dst) in enumerate(
+        (
+            ("pool", pool_in, pool),
+            ("w_key", w_key_in, w_key),
+            ("w_value", w_value_in, w_value),
+            ("table_row", table_in, table_row),
+            ("source_row", source_in, source_row),
+            ("table", table_in, table),
+            ("source", source_in, source),
+            ("drawn", drawn_in, drawn),
+            ("weight", weight_in, weight),
+            ("cotangent", cotangent_in, cotangent),
+            ("w_query", w_query_in, w_query),
+            ("q_gain", q_gain_in, q_gain),
+            ("k_gain", k_gain_in, k_gain),
+        )
+    ):
+        loads[name] = pltpu.make_async_copy(src, dst, load_s.at[i])
+        loads[name].start()
+
+    for name in ("pool", "w_key", "w_value"):
+        loads[name].wait()
+    rows = pool[...].reshape(TOKENS, WIDTH).astype(F32)
+    x_ref[:COLS] = rows[:, :COLS].T.astype(BF16)
+    rest = [rows[:, COLS:], jnp.zeros((TOKENS, PADDED - WIDTH), F32)]
+    x_ref[COLS:] = jnp.concatenate(rest, axis=1).T.astype(BF16)
+    rows = pl.ds(pl.multiple_of(x * SHARE, 16), SHARE)
+    for which, w_ref in ((0, w_key), (1, w_value)):
+
+        @pl.when(core == which)
+        def _():
+            for g in range(N_Y):
+                w_mine[g] = w_ref[rows, g * HEAD : (g + 1) * HEAD]
+
+    loads["table_row"].wait()
+    loads["source_row"].wait()
+    pl.semaphore_wait(barrier, len(partners))
 
     def block(step_y, step_z):
         return lax.rem(y + step_y, N_Y) * N_ZL + lax.rem(zl + step_z, N_ZL)
@@ -179,21 +263,71 @@
     for way, step in ((0, 1), (1, N_Y - 1)):
         start(tokens, piece.at[mp], ty_s.at[0, way], ty_r.at[0, way], at_y(step))
 
-    rows = pl.ds(pl.multiple_of(x * SHARE, 16), SHARE)
     w_kv[core, mp, rows] = w_mine[y]
     for step in range(1, N_MP):
         dest = at_mp(step)
         start(w_mine.at[dest[1] // N_ZL], w_kv.at[core, mp, rows], w1_s, w1_r, dest)
 
-    for k in range(N_DP):
-        wanted = lax.rem(dp + k, N_DP)
-        slot = jnp.int32(SEQS)
+    for k in (1, 2, 3):
+        start(table_row, tables.at[k], ts_s.at[k, 0], ts_r.at[k, 0], at_zh(N_ZH - k))
+        start(source_row, sources.at[k], ts_s.at[k, 1], ts_r.at[k, 1], at_zh(N_ZH - k))
+
+    def line_send(buf, send, recv):
+        for way, step in ((0, 1), (1, N_ZH - 1)):
+            start(
+                buf[0].at[pl.ds(0, SEQS)],
+                buf[N_ZH - 1 if way == 0 else 1].at[pl.ds(0, SEQS)],
+                send.at[way],
+                recv.at[way],
+                at_zh(step),
+            )
+
+    def line_pass(buf, send, recv, send_on, recv_on):
+        for way, step in ((0, 1), (1, N_ZH - 1)):
+            k = N_ZH - 1 if way == 0 else 1
+            spot = buf[k].at[pl.ds(0, SEQS)]
+            copy(spot, spot, send.at[way], recv.at[way], at_zh(step)).wait_recv()
+            some = pl.ds(way * (SEQS // 2), SEQS // 2)
+            start(
+                buf[k].at[some],
+                buf[2].at[some],
+                send_on.at[way],
+                recv_on.at[way],
+                at_zh(step),
+            )
+
+    def line_end(buf, send_on, recv_on):
+        for way in (0, 1):
+            spot = buf[2].at[pl.ds(way * (SEQS // 2), SEQS // 2)]
+            copy(spot, spot, send_on.at[way], recv_on.at[way], at_zh(1)).wait_recv()
+
+    def deal(buf, k, pick, out, into, send, recv):
+        for i, (step, flip) in enumerate(PAIRS):
+            to = pair(step, flip)
+            out[i, k] = buf[k][pick(k, to)]
+            start(out.at[i, k], into.at[i, k], send, recv, (to, mp))
+        into[len(PAIRS), k] = buf[k][pick(k, dp)]
+
+    def dealt(into, send, recv):
+        spot = into.at[pl.ds(0, len(PAIRS))]
+        copy(spot, spot, send, recv, sibling).wait_recv()
+
+    for name in ("drawn", "weight", "cotangent", "table", "source"):
+        loads[name].wait()
+    for s in range(SEQS):
+        factor = drawn[s].astype(F32) * weight[s] * (1.0 / LENGTH)
+        d_all[0][s] = (cotangent[s].astype(F32) * factor).astype(BF16)
+    for k in range(N_ZH):
+        d_all[k][SEQS] = jnp.zeros((LENGTH, COLS), BF16)
+
+    def slot_of(k, rank):
+        found = jnp.int32(SEQS)
         for s in range(SEQS):
-            slot = jnp.where(source[s] == wanted, jnp.int32(s), slot)
-        d_send[k] = d_out[slot]
-        if k:
-            start(d_send.at[k], d_slots.at[k], co_s, co_r, at_dp(k))
-    d_slots[0] = d_send[0]
+            have = source[s] if k == 0 else near_sources[k, s]
+            found = jnp.where(have == rank, jnp.int32(s), found)
+        return found
+
+    deal(d_all, 0, slot_of, d_send, d_slots, c2_s, c2_r)
 
     acc_q[...] = jnp.zeros_like(acc_q)
 
@@ -217,45 +351,79 @@
         for way, step in ((0, 1), (1, N_Y - 1)):
             start(spot, spot, ty_s.at[k, way], ty_r.at[k, way], at_y(step))
 
+    loads["w_query"].wait()
+    def w_rows(step):
+        at = lax.rem(x + step, N_X) * SHARE
+        return w_kv.at[core, :, pl.ds(pl.multiple_of(at, 16), SHARE)]
+
+    def w_across(step):
+        spot = w_rows(step)
+        start(spot, spot, w3_s.at[step], w3_r.at[step], sibling)
+
+    def w_arrived(step):
+        spot = w_rows(N_X - step)
+        copy(spot, spot, w2_s.at[step], w2_r.at[step], at_x(step)).wait_recv()
+        w_across(N_X - step)
+
     project(mp)
     take(1)
     project(mine(1))
+    got = w_kv.at[0, pl.ds(0, N_MP - 1), pl.ds(0, SHARE)]
+    copy(got, got, w1_s, w1_r, at_mp(1)).wait_recv()
+    for k in (1, 3, 2):
+        start(w_rows(0), w_rows(0), w2_s.at[k], w2_r.at[k], at_x(k))
+    w_across(0)
     pass_on(0)
     take(2)
     project(mine(2))
     take(3)
+    line_send(d_all, c1_s, c1_r)
     project(mine(3))
-    got = w_kv.at[0, pl.ds(0, N_MP - 1), pl.ds(0, SHARE)]
-    copy(got, got, w1_s, w1_r, at_mp(1)).wait_recv()
-    part = w_kv.at[core, :, rows]
-    for k in (1, 2, 3):
-        start(part, part, w2_s.at[k], w2_r.at[k], at_x(k))
     for way in (0, 1):
         project(near(0, way))
-    for k in (1, 2, 3):
-        pass_on(k)
+    pass_on(1)
+    w_arrived(1)
+    w_arrived(3)
+    pass_on(2)
+    w_arrived(2)
+    pass_on(3)
+    for k in (1, 2, 3):
         for way in (0, 1):
             project(near(k, way))
     for k in (1, 2, 3):
-        copy(part, part, w2_s.at[k], w2_r.at[k], at_x(k)).wait_recv()
-    start(w_kv.at[core], w_kv.at[core], w3_s, w3_r, sibling)
+        for i, row, rows in ((0, table_row, tables), (1, source_row, sources)):
+            copy(
+                row, rows.at[k], ts_s.at[k, i], ts_r.at[k, i], at_zh(k)
+            ).wait_recv()
+    fetch = pltpu.make_async_copy(tables, near_tables, load_s.at[13])
+    fetch.start()
+    fetch.wait()
+    fetch = pltpu.make_async_copy(sources, near_sources, load_s.at[14])
+    fetch.start()
+    fetch.wait()
+    line_pass(d_all, c1_s, c1_r, cf_s, cf_r)
+    for k in (1, 3):
+        deal(d_all, k, slot_of, d_send, d_slots, c2_s, c2_r)
     for k in range(N_ZL):
         far = block(2, N_ZL - k if k else 0)
         for way in (0, 1):
             half = piece.at[far, pl.ds(way * HALF, HALF)]
             copy(half, half, tf_s.at[k, way], tf_r.at[k, way], at_y(1)).wait_recv()
         project(far)
-    copy(w_kv.at[other], w_kv.at[other], w3_s, w3_r, sibling).wait_recv()
-    acc_kv[...] = jnp.zeros_like(acc_kv)
-
-    def project_kv(j, carry):
-        for half in (0, 1):
-            acc_kv[half] += dot_tn(w_kv[half, j], piece[j])
-        return carry
-
-    lax.fori_loop(0, N_MP, project_kv, 0)
-
-    gain_q, gain_k = q_gain[...], k_gain[...]
+    for k in range(N_X):
+        at = lax.rem(x + k, N_X) * SHARE
+        spot = w_kv.at[other, :, pl.ds(pl.multiple_of(at, 16), SHARE)]
+        copy(spot, spot, w3_s.at[k], w3_r.at[k], sibling).wait_recv()
+    gathered = piece[...].reshape(N_MP * WIDTH, TOKENS)
+    for half in (0, 1):
+        w_half = w_kv[half].reshape(N_MP * WIDTH, HEAD)
+        acc_kv[half] = dot_tn(w_half, gathered)
+
+    loads["q_gain"].wait()
+    loads["k_gain"].wait()
+    gain_q, gain_k = (
+        jnp.broadcast_to(gain[...], (HEAD, HEAD)).T[:, :1] for gain in (q_gain, k_gain)
+    )
     key_sum = acc_kv[0]
     k_inverse = lax.rsqrt(jnp.mean(key_sum * key_sum, axis=0, keepdims=True) + EPS)
     k_norm = (key_sum * k_inverse * gain_k).astype(BF16)
@@ -273,19 +441,34 @@
         probs = raised / jnp.sum(raised, axis=0, keepdims=True)
         p_half = probs.astype(BF16)
         out = dot_nn(value, p_half).T.astype(BF16)
-        att[:, :, h * HEAD : (h + 1) * HEAD] = out.reshape(SEQS, LENGTH, HEAD)
+        att_all[0][:, :, h * HEAD : (h + 1) * HEAD] = out.reshape(SEQS, LENGTH, HEAD)
         saved.append((query, inverse, q_norm, probs, p_half))
-    for k in range(N_DP):
-        spot = table[0, lax.rem(dp + k, N_DP)]
-        att_send[k] = att[jnp.maximum(spot, 0)]
-        if k:
-            start(att_send.at[k], att_slots.at[k], at_s, at_r, at_dp(k))
-    att_slots[0] = att_send[0]
-
-    got = d_slots.at[pl.ds(1, N_DP - 1)]
-    copy(got, got, co_s, co_r, at_dp(1)).wait_recv()
+    def sent_to(k, rank):
+        have = table[0, rank] if k == 0 else near_tables[k, 0, rank]
+        return jnp.maximum(have, 0)
+
+    line_send(att_all, a1_s, a1_r)
+    deal(att_all, 0, sent_to, att_send, att_slots, a2_s, a2_r)
+
+    line_end(d_all, cf_s, cf_r)
+    deal(d_all, 2, slot_of, d_send, d_slots, c2_s, c2_r)
+    dealt(d_slots, c2_s, c2_r)
+    lane = lax.broadcasted_iota(jnp.int32, (1, N_DP * LENGTH), 1)
+    target = jnp.zeros_like(lane)
+
+    def sender(step, flip, k):
+        of_x = lax.rem(x + N_X - step, N_X)
+        of_core = other if flip else core
+        return of_x * (N_ZH * N_CORE) + lax.rem(zh + k, N_ZH) * N_CORE + of_core
+
+    for i, (step, flip) in enumerate(PAIRS + ((0, 0),)):
+        for k in range(N_ZH):
+            entry = table[0, sender(step, flip, k)]
+            here = (lane >> 5) == i * N_ZH + k
+            target = jnp.where(here, entry * LENGTH, target)
+    target = jnp.where(target < 0, -1, target + (lane & (LENGTH - 1)))
     place = lax.broadcasted_iota(jnp.int32, (TOKENS, N_DP * LENGTH), 0)
-    chosen = jnp.where(place == target[...], 1.0, 0.0).astype(BF16)
+    chosen = jnp.where(place == target, 1.0, 0.0).astype(BF16)
     d_rows = dot_nn(chosen, d_slots[...].reshape(N_DP * LENGTH, COLS))
     d_cols = d_rows.T.astype(BF16)
     d_knorm = jnp.zeros((HEAD, TOKENS), F32)
@@ -319,13 +502,10 @@
         )
 
     def partial_rows(to, into, which):
-        def one(i, carry):
-            rows = pl.ds(pl.multiple_of(which * HALF, 16), HALF)
-            total = dot_nn(piece[to * N_ZH + i, rows], d_query[...])
-            into[to, i] = total.astype(BF16)
-            return carry
-
-        lax.fori_loop(0, N_ZH, one, 0)
+        rows = pl.ds(pl.multiple_of(which * HALF, 16), HALF)
+        found = piece[pl.ds(to * N_ZH, N_ZH), rows].reshape(N_ZH * HALF, TOKENS)
+        total = dot_nn(found, d_query[...]).astype(BF16)
+        into[to] = total.reshape(N_ZH, HALF, COLS)
 
     def x_at(step):
         return lax.rem(x + step, N_X)
@@ -368,6 +548,10 @@
                     at_x(k),
                 )
 
+    line_pass(att_all, a1_s, a1_r, af_s, af_r)
+    for k in (1, 3):
+        deal(att_all, k, sent_to, att_send, att_slots, a2_s, a2_r)
+
     for k in (1, 2, 3):
         copy(spot, spot, k2_s.at[k], k2_r.at[k], at_zl(k)).wait_recv()
     group = dkv_all.at[y]
@@ -376,7 +560,7 @@
     for k in (1, 2, 3):
         copy(group, group, k3_s.at[k], k3_r.at[k], at_y(k)).wait_recv()
 
-    def kv_rows(g, carry):
+    for g in range(N_X):
         rows = dkv_all[g].reshape(2 * HEAD, TOKENS)
         product = dot_nt(rows, x_ref[...]).astype(BF16)
         for half in range(2):
@@ -384,9 +568,6 @@
                 for c in range(N_CORE):
                     first = half * HEAD + i * 32 + c * 16
                     kv_part[c, g, i, half] = product[first : first + 16]
-        return carry
-
-    lax.fori_loop(0, N_X, kv_rows, 0)
     start(kv_part.at[other], kv_recv, vc_s, vc_r, sibling)
 
     for kz in order:
@@ -402,6 +583,8 @@
                 z_send.at[to_z], z_recv.at[kz], gz_s.at[kz], gz_r.at[kz], at_zh(kz)
             )
 
+    line_end(att_all, af_s, af_r)
+    deal(att_all, 2, sent_to, att_send, att_slots, a2_s, a2_r)
     copy(kv_part.at[other], kv_recv, vc_s, vc_r, sibling).wait_recv()
     kv_sum[...] = (kv_part[core].astype(F32) + kv_recv[...].astype(F32)).astype(BF16)
     for k in (1, 2, 3):
@@ -425,13 +608,17 @@
     for k in (1, 2, 3):
         copy(kv_zs.at[0], kv_z.at[k], vz_s.at[k], vz_r.at[k], at_zh(k)).wait_recv()
         total += kv_z[k].astype(F32)
-    gkv_out[...] = total
-
-    got = att_slots.at[pl.ds(1, N_DP - 1)]
-    copy(got, got, at_s, at_r, at_dp(1)).wait_recv()
+    gk_out[...] = total[0][:, :WIDTH]
+    gv_out[...] = total[1][:, :WIDTH]
+
+    dealt(att_slots, a2_s, a2_r)
     for s in range(SEQS):
-        att_out[s] = att_slots[lax.rem(dp + N_DP - source[s], N_DP)]
-
+        rank = source[s]
+        step = lax.rem(x + N_X - rank // (N_ZH * N_CORE), N_X)
+        flip = lax.rem(rank + core, N_CORE)
+        k = lax.rem((rank // N_CORE) % N_ZH + N_ZH - zh, N_ZH)
+        place = lax.rem(step * N_CORE + flip + len(PAIRS), len(PAIRS) + 1)
+        att_out[s] = att_slots[place, k]
     for made in sends:
         made.wait_send()
 
@@ -449,43 +636,51 @@
     query_gain,
     key_gain,
 ):
-    dp = lax.axis_index("dp")
-    rank_x, core = dp // (N_ZH * N_CORE), dp % N_CORE
-    rows = pool.reshape(TOKENS, WIDTH).T
-    rows = jnp.pad(rows, ((0, PADDED - WIDTH), (0, 0)))
-    weights = jnp.where(core == 0, w_key, w_value)
-    weights = lax.dynamic_slice_in_dim(weights, rank_x * SHARE, SHARE, 0)
-    weights = weights.reshape(SHARE, N_Y, HEAD).transpose(1, 0, 2)
-    factor = multiplicity.astype(F32) * slot_weight / LENGTH
-    d_out = (cotangent.astype(F32) * factor[:, None, None]).astype(BF16)
-    d_out = jnp.pad(d_out, ((0, 1), (0, 0), (0, 0)))
-    entry = send_table[0, (dp + N_DP - jnp.arange(N_DP)) % N_DP]
-    target = jnp.where(
-        entry[:, None] >= 0, entry[:, None] * LENGTH + jnp.arange(LENGTH)[None, :], -1
-    ).reshape(1, N_DP * LENGTH)
-
     dma = pltpu.SemaphoreType.DMA
-    smem = pl.BlockSpec(memory_space=pltpu.SMEM)
     vmem = pl.BlockSpec(memory_space=pltpu.VMEM)
-    attended, grad_query, grad_kv = pl.pallas_call(
+    attended, grad_query, grad_key, grad_value = pl.pallas_call(
         kernel,
         out_shape=(
             jax.ShapeDtypeStruct((SEQS, LENGTH, COLS), BF16),
             jax.ShapeDtypeStruct((HALF, COLS), F32),
-            jax.ShapeDtypeStruct((2, 16, PADDED), F32),
+            jax.ShapeDtypeStruct((16, WIDTH), F32),
+            jax.ShapeDtypeStruct((16, WIDTH), F32),
         ),
-        in_specs=[smem, smem] + [vmem] * 7,
-        out_specs=(vmem, vmem, vmem),
+        in_specs=[pl.BlockSpec(memory_space=pl.ANY)] * 11,
+        out_specs=(vmem,) * 4,
         scratch_shapes=[
+            pltpu.SMEM((1, N_DP), jnp.int32),
+            pltpu.SMEM((SEQS,), jnp.int32),
+            pltpu.SMEM((SEQS,), jnp.int32),
+            pltpu.SMEM((SEQS,), F32),
+            pltpu.VMEM((SEQS, LENGTH, WIDTH), BF16),
+            pltpu.VMEM((SEQS, LENGTH, COLS), BF16),
+            pltpu.VMEM((N_MP * WIDTH, COLS), BF16),
+            pltpu.VMEM((WIDTH, N_Y * HEAD), BF16),
+            pltpu.VMEM((WIDTH, N_Y * HEAD), BF16),
+            pltpu.VMEM((1, HEAD), F32),
+            pltpu.VMEM((1, HEAD), F32),
+            dma((15,)),
+            pltpu.VMEM((1, N_DP), jnp.int32),
+            pltpu.VMEM((SEQS,), jnp.int32),
+            pltpu.VMEM((N_ZH, 1, N_DP), jnp.int32),
+            pltpu.VMEM((N_ZH, SEQS), jnp.int32),
+            pltpu.SMEM((N_ZH, 1, N_DP), jnp.int32),
+            pltpu.SMEM((N_ZH, SEQS), jnp.int32),
+            dma((4, 2)),
+            dma((4, 2)),
+            pltpu.VMEM((PADDED, TOKENS), BF16),
+            pltpu.VMEM((N_Y, SHARE, HEAD), BF16),
             pltpu.VMEM((N_MP, WIDTH, TOKENS), BF16),
             pltpu.VMEM((2, N_MP, WIDTH, HEAD), BF16),
-            pltpu.VMEM((N_DP, LENGTH, COLS), BF16),
-            pltpu.VMEM((N_DP, LENGTH, COLS), BF16),
+            *[pltpu.VMEM((SEQS + 1, LENGTH, COLS), BF16)] * N_ZH,
+            pltpu.VMEM((len(PAIRS), N_ZH, LENGTH, COLS), BF16),
+            pltpu.VMEM((len(PAIRS) + 1, N_ZH, LENGTH, COLS), BF16),
             pltpu.VMEM((COLS, TOKENS), F32),
             pltpu.VMEM((2, HEAD, TOKENS), F32),
-            pltpu.VMEM((SEQS, LENGTH, COLS), BF16),
-            pltpu.VMEM((N_DP, LENGTH, COLS), BF16),
-            pltpu.VMEM((N_DP, LENGTH, COLS), BF16),
+            *[pltpu.VMEM((SEQS, LENGTH, COLS), BF16)] * N_ZH,
+            pltpu.VMEM((len(PAIRS), N_ZH, LENGTH, COLS), BF16),
+            pltpu.VMEM((len(PAIRS) + 1, N_ZH, LENGTH, COLS), BF16),
             pltpu.VMEM((TOKENS, COLS), BF16),
             pltpu.VMEM((N_X, N_ZH, HALF, COLS), BF16),
             pltpu.VMEM((N_X, N_ZH, HALF, COLS), BF16),
@@ -512,48 +707,57 @@
             dma,
             dma((4,)),
             dma((4,)),
+            dma((4,)),
+            dma((4,)),
+            dma((2,)),
+            dma((2,)),
+            dma((2,)),
+            dma((2,)),
             dma,
             dma,
+            dma((2,)),
+            dma((2,)),
+            dma((2,)),
+            dma((2,)),
             dma,
             dma,
+            dma((4,)),
+            dma((4,)),
+            dma((4,)),
+            dma((4,)),
+            dma((4,)),
+            dma((4,)),
+            dma((4,)),
+            dma((4,)),
+            dma((4, 4)),
+            dma((4, 4)),
+            dma((4,)),
+            dma((4,)),
             dma,
             dma,
             dma((4,)),
             dma((4,)),
             dma((4,)),
             dma((4,)),
-            dma((4,)),
-            dma((4,)),
-            dma((4,)),
-            dma((4,)),
-            dma((4, 4)),
-            dma((4, 4)),
-            dma((4,)),
-            dma((4,)),
-            dma,
-            dma,
-            dma((4,)),
-            dma((4,)),
-            dma((4,)),
-            dma((4,)),
         ],
         compiler_params=pltpu.CompilerParams(
-            collective_id=0, has_side_effects=True, vmem_limit_bytes=48 * 1024 * 1024
+            collective_id=0, has_side_effects=True, vmem_limit_bytes=60 * 1024 * 1024
         ),
         name="train_step",
     )(
         send_table,
         slot_source,
-        rows,
-        weights,
+        multiplicity,
+        slot_weight,
+        pool,
+        cotangent,
         w_query,
-        d_out,
-        target,
-        query_gain[:, None],
-        key_gain[:, None],
+        w_key,
+        w_value,
+        query_gain.reshape(1, HEAD),
+        key_gain.reshape(1, HEAD),
     )
-    key_gradient, grad_value = grad_kv[0, :, :WIDTH].T, grad_kv[1, :, :WIDTH].T
-    return attended, grad_query, key_gradient, grad_value
+    return attended, grad_query, grad_key.T, grad_value.T
 
 
 def solution(mesh):

time: 162 us -> 125 us (0.77)
  Pallas kernels: 149 us -> 118 us
  local copies, waits for them, and re-layouts: 9.01 us -> 5.85 us
  other arithmetic: 2.73 us -> 0 us
    pallas_call x1, Pallas kernels: 149 us -> 118 us  [local(): pl.pallas_call(kernel, out_shape=(jax.ShapeDtypeStruct((SEQS, LENGTH, COL...]
    unnamed x8 -> x4, local copies, waits for them, and re-layouts: 4.37 us -> 5.85 us
where the time goes in v2:
time: 125 us; the launch traced here: 124 us
  Pallas kernels  118 us (94%)
  local copies, waits for them, and re-layouts  5.85 us (5%)
    pallas_call x1, Pallas kernels, local(): pl.pallas_call(kernel, out_shape=(jax.ShapeDtypeStruct((SEQS, LENGTH, COL...  118 us
    unnamed x4, local copies, waits for them, and re-layouts  5.85 us

profile of v2, /device:TPU:1, one launch (start us, length us, event | category | flops | bytes accessed | tf_op | source)
XLA Modules:
  0.0 124.3 jit_solution(10658699672750389288)
XLA Ops:
  0.6 117.8 %train_step.1 = (bf16[8,32,256]{2,1,0:T(8,128)(2,1)}, f32[160,256]{1,0:T(8,128)}, f32[16,320]{1,0:T(8,128)}, f32[16,320]{1,0:T(8,128)}) custom-call(s32[1,32]{1,0:T(1,128)} %table_in.1, s32[8]{0:T(128)} %source_in.1, s32[8]{0:T(128)} %drawn_in.1, f32[8]{0:T(128)} %weight_in.1, bf16[8,32,320]{2,1,0:T(8,128)(2,1)} %pool_in.1, ...), custom_call_target="tpu_custom_call" | custom-call | tf_op jit(solution)/shard_map/train_step/pallas_call | solution.py:641
  118.4 1.6 %copy.19 = bf16[8,32,256]{2,1,0:T(8,128)(2,1)} copy(bf16[8,32,256]{2,1,0:T(8,128)(2,1)} %get-tuple-element.16) | data formatting | bytes 262144
  120.0 1.6 %copy.20 = f32[160,256]{1,0:T(8,128)} copy(f32[160,256]{1,0:T(8,128)} %get-tuple-element.17) | data formatting | bytes 327680
  121.6 1.3 %copy.21 = f32[320,16]{0,1:T(8,128)} copy(f32[320,16]{0,1:T(8,128)} %bitcast.5) | data formatting | bytes 40960
  122.9 1.3 %copy.22 = f32[320,16]{0,1:T(8,128)} copy(f32[320,16]{0,1:T(8,128)} %bitcast.4) | data formatting | bytes 40960

commit v3 on v2

--- a/solution.py
+++ b/solution.py
@@ -247,54 +247,80 @@
     loads["source_row"].wait()
     pl.semaphore_wait(barrier, len(partners))
 
-    def block(step_y, step_z):
-        return lax.rem(y + step_y, N_Y) * N_ZL + lax.rem(zl + step_z, N_ZL)
-
-    def mine(step):
-        return block(0, N_ZL - step)
+    fellow = zl + 1 - 2 * (zl % 2)
+    across = N_ZL - 1 - zl
+    inner = (zl == 1) | (zl == 2)
+    line_of = (
+        zl,
+        fellow,
+        jnp.where(zl < 2, jnp.int32(2), jnp.int32(1)),
+        jnp.where(zl < 2, jnp.int32(3), jnp.int32(0)),
+    )
+
+    def mine(k):
+        return y * N_ZL + line_of[k]
 
     def near(k, way):
-        return block(N_Y - 1 if way == 0 else 1, N_ZL - k if k else 0)
+        return lax.rem(y + (N_Y - 1 if way == 0 else 1), N_Y) * N_ZL + line_of[k]
+
+    inner_sends = []
+
+    def start_inner(*args):
+        inner_sends.append(args)
+
+        @pl.when(inner)
+        def _():
+            copy(*args).start()
+
+    def along_y(k):
+        spot = piece.at[mine(k)]
+        for way, step in ((0, 1), (1, N_Y - 1)):
+            start(spot, spot, ty_s.at[k, way], ty_r.at[k, way], at_y(step))
 
     piece[mp] = x_ref[:WIDTH]
-    tokens = x_ref.at[pl.ds(0, WIDTH)]
-    for k in (1, 2, 3):
-        start(tokens, piece.at[mp], tz_s.at[k], tz_r.at[k], at_zl(k))
-    for way, step in ((0, 1), (1, N_Y - 1)):
-        start(tokens, piece.at[mp], ty_s.at[0, way], ty_r.at[0, way], at_y(step))
-
     w_kv[core, mp, rows] = w_mine[y]
     for step in range(1, N_MP):
         dest = at_mp(step)
         start(w_mine.at[dest[1] // N_ZL], w_kv.at[core, mp, rows], w1_s, w1_r, dest)
+    tokens = piece.at[mp]
+    start(tokens, tokens, tz_s.at[0], tz_r.at[1], (dp, y * N_ZL + fellow))
+    start_inner(tokens, tokens, tz_s.at[1], tz_r.at[2], (dp, y * N_ZL + across))
+    along_y(0)
 
     for k in (1, 2, 3):
         start(table_row, tables.at[k], ts_s.at[k, 0], ts_r.at[k, 0], at_zh(N_ZH - k))
         start(source_row, sources.at[k], ts_s.at[k, 1], ts_r.at[k, 1], at_zh(N_ZH - k))
 
+    half_slots = SEQS // 2
+
     def line_send(buf, send, recv):
-        for way, step in ((0, 1), (1, N_ZH - 1)):
-            start(
-                buf[0].at[pl.ds(0, SEQS)],
-                buf[N_ZH - 1 if way == 0 else 1].at[pl.ds(0, SEQS)],
-                send.at[way],
-                recv.at[way],
-                at_zh(step),
-            )
+        for part in (0, 1):
+            for way, step in ((0, 1), (1, N_ZH - 1)):
+                some = pl.ds((way ^ part) * half_slots, half_slots)
+                start(
+                    buf[0].at[some],
+                    buf[N_ZH - 1 if way == 0 else 1].at[some],
+                    send.at[way, part],
+                    recv.at[way, part],
+                    at_zh(step),
+                )
 
     def line_pass(buf, send, recv, send_on, recv_on):
-        for way, step in ((0, 1), (1, N_ZH - 1)):
-            k = N_ZH - 1 if way == 0 else 1
-            spot = buf[k].at[pl.ds(0, SEQS)]
-            copy(spot, spot, send.at[way], recv.at[way], at_zh(step)).wait_recv()
-            some = pl.ds(way * (SEQS // 2), SEQS // 2)
-            start(
-                buf[k].at[some],
-                buf[2].at[some],
-                send_on.at[way],
-                recv_on.at[way],
-                at_zh(step),
-            )
+        for part in (0, 1):
+            for way, step in ((0, 1), (1, N_ZH - 1)):
+                some = pl.ds((way ^ part) * half_slots, half_slots)
+                spot = buf[N_ZH - 1 if way == 0 else 1].at[some]
+                copy(
+                    spot, spot, send.at[way, part], recv.at[way, part], at_zh(step)
+                ).wait_recv()
+                if part == 0:
+                    start(
+                        spot,
+                        buf[2].at[some],
+                        send_on.at[way],
+                        recv_on.at[way],
+                        at_zh(step),
+                    )
 
     def line_end(buf, send_on, recv_on):
         for way in (0, 1):
@@ -347,11 +373,13 @@
 
     def take(k):
         spot = piece.at[mine(k)]
-        copy(spot, spot, tz_s.at[k], tz_r.at[k], at_zl(1)).wait_recv()
-        for way, step in ((0, 1), (1, N_Y - 1)):
-            start(spot, spot, ty_s.at[k, way], ty_r.at[k, way], at_y(step))
-
-    loads["w_query"].wait()
+        copy(spot, spot, tz_s.at[k], tz_r.at[k], at_y(1)).wait_recv()
+        to = across if k == 1 else fellow
+        start_inner(
+            spot, spot, tz_s.at[k + 1], tz_r.at[3 if k == 1 else k], (dp, y * N_ZL + to)
+        )
+        along_y(k)
+
     def w_rows(step):
         at = lax.rem(x + step, N_X) * SHARE
         return w_kv.at[core, :, pl.ds(pl.multiple_of(at, 16), SHARE)]
@@ -365,51 +393,61 @@
         copy(spot, spot, w2_s.at[step], w2_r.at[step], at_x(step)).wait_recv()
         w_across(N_X - step)
 
+    def far_arrived(k):
+        far = lax.rem(y + 2, N_Y) * N_ZL + line_of[k]
+        for way in (0, 1):
+            half = piece.at[far, pl.ds(way * HALF, HALF)]
+            copy(half, half, tf_s.at[k, way], tf_r.at[k, way], at_y(1)).wait_recv()
+        project(far)
+
+    loads["w_query"].wait()
     project(mp)
     take(1)
-    project(mine(1))
+    pass_on(0)
     got = w_kv.at[0, pl.ds(0, N_MP - 1), pl.ds(0, SHARE)]
     copy(got, got, w1_s, w1_r, at_mp(1)).wait_recv()
     for k in (1, 3, 2):
         start(w_rows(0), w_rows(0), w2_s.at[k], w2_r.at[k], at_x(k))
     w_across(0)
-    pass_on(0)
-    take(2)
-    project(mine(2))
-    take(3)
-    line_send(d_all, c1_s, c1_r)
-    project(mine(3))
+    project(mine(1))
     for way in (0, 1):
         project(near(0, way))
+    take(2)
+    line_send(d_all, c1_s, c1_r)
+    project(mine(2))
     pass_on(1)
+    take(3)
+    project(mine(3))
+    far_arrived(0)
+    pass_on(2)
     w_arrived(1)
     w_arrived(3)
-    pass_on(2)
-    w_arrived(2)
-    pass_on(3)
-    for k in (1, 2, 3):
+    for k in (1, 2):
         for way in (0, 1):
             project(near(k, way))
+    pass_on(3)
+    w_arrived(2)
+    for way in (0, 1):
+        project(near(3, way))
+    far_arrived(1)
+    far_arrived(2)
     for k in (1, 2, 3):
         for i, row, rows in ((0, table_row, tables), (1, source_row, sources)):
             copy(
                 row, rows.at[k], ts_s.at[k, i], ts_r.at[k, i], at_zh(k)
             ).wait_recv()
-    fetch = pltpu.make_async_copy(tables, near_tables, load_s.at[13])
-    fetch.start()
-    fetch.wait()
-    fetch = pltpu.make_async_copy(sources, near_sources, load_s.at[14])
-    fetch.start()
-    fetch.wait()
+    fetches = [
+        pltpu.make_async_copy(tables, near_tables, load_s.at[13]),
+        pltpu.make_async_copy(sources, near_sources, load_s.at[14]),
+    ]
+    for fetch in fetches:
+        fetch.start()
+    for fetch in fetches:
+        fetch.wait()
     line_pass(d_all, c1_s, c1_r, cf_s, cf_r)
     for k in (1, 3):
         deal(d_all, k, slot_of, d_send, d_slots, c2_s, c2_r)
-    for k in range(N_ZL):
-        far = block(2, N_ZL - k if k else 0)
-        for way in (0, 1):
-            half = piece.at[far, pl.ds(way * HALF, HALF)]
-            copy(half, half, tf_s.at[k, way], tf_r.at[k, way], at_y(1)).wait_recv()
-        project(far)
+    far_arrived(3)
     for k in range(N_X):
         at = lax.rem(x + k, N_X) * SHARE
         spot = w_kv.at[other, :, pl.ds(pl.multiple_of(at, 16), SHARE)]
@@ -501,23 +539,102 @@
             at_zl(k),
         )
 
+    def x_at(step):
+        return lax.rem(x + step, N_X)
+
+    def zh_at(step):
+        return lax.rem(zh + step, N_ZH)
+
     def partial_rows(to, into, which):
         rows = pl.ds(pl.multiple_of(which * HALF, 16), HALF)
-        found = piece[pl.ds(to * N_ZH, N_ZH), rows].reshape(N_ZH * HALF, TOKENS)
-        total = dot_nn(found, d_query[...]).astype(BF16)
-        into[to] = total.reshape(N_ZH, HALF, COLS)
-
-    def x_at(step):
-        return lax.rem(x + step, N_X)
+        for i in range(N_X):
+            total = dot_nn(piece[i * N_ZH + to, rows], d_query[...])
+            into[to, i] = total.astype(BF16)
+
+    def core_step(kz):
+        to = zh_at(kz)
+        copy(
+            g_send.at[to], g_recv.at[to], gc_s.at[kz], gc_r.at[kz], sibling
+        ).wait_recv()
+        both = g_keep[to].astype(F32) + g_recv[to].astype(F32)
+        g_keep[to] = both.astype(BF16)
+        for k in (2, 1, 3):
+            start(
+                g_keep.at[to, x_at(k)],
+                x_recv.at[to, k],
+                gx_s.at[k, kz],
+                gx_r.at[k, kz],
+                at_x(k),
+            )
+
+    def x_step(kz):
+        to = zh_at(kz)
+        total = g_keep[to, x].astype(F32)
+        for k in (1, 2, 3):
+            spot = x_recv.at[to, k]
+            copy(spot, spot, gx_s.at[k, kz], gx_r.at[k, kz], at_x(k)).wait_recv()
+            total += x_recv[to, k].astype(F32)
+        z_send[to] = total.astype(BF16)
+        if kz:
+            start(z_send.at[to], z_recv.at[kz], gz_s.at[kz], gz_r.at[kz], at_zh(kz))
 
     order = (2, 1, 3, 0)
-    for k in order:
-        to = x_at(k)
+
+    def kv_place(i):
+        step = lax.rem(i + N_ZH - zh, N_ZH)
+        return jnp.where(
+            step == 0, 3, jnp.where(step == 1, 1, jnp.where(step == 2, 0, 2))
+        )
+
+    def kv_core_step(part):
+        some = pl.ds(2 * part, 2)
+        copy(
+            kv_part.at[other, some],
+            kv_recv.at[some],
+            vc_s.at[part],
+            vc_r.at[part],
+            sibling,
+        ).wait_recv()
+        both = kv_part[core, some].astype(F32) + kv_recv[some].astype(F32)
+        both = both.astype(BF16)
+        for g in range(N_X):
+            kv_sum[g, some] = both[:, g]
+        for k in (2, 1, 3):
+            start(
+                kv_sum.at[x_at(k), some],
+                kv_x.at[k, some],
+                vx_s.at[k, part],
+                vx_r.at[k, part],
+                at_x(k),
+            )
+
+    def kv_x_step(part):
+        some = pl.ds(2 * part, 2)
+        total = kv_sum[x, some].astype(F32)
+        for k in (1, 2, 3):
+            spot = kv_x.at[k, some]
+            copy(
+                spot, spot, vx_s.at[k, part], vx_r.at[k, part], at_x(k)
+            ).wait_recv()
+            total += kv_x[k, some].astype(F32)
+        kv_zs[some] = total.astype(BF16)
+        for p in (0, 1):
+            k = order[2 * part + p]
+            if k:
+                start(
+                    kv_zs.at[2 * part + p],
+                    kv_z.at[k],
+                    vz_s.at[k],
+                    vz_r.at[k],
+                    at_zh(k),
+                )
+
+    for kz in order:
+        to = zh_at(kz)
         partial_rows(to, g_send, other)
-        start(g_send.at[to], g_recv.at[to], gc_s.at[k], gc_r.at[k], sibling)
-    for k in order:
-        partial_rows(x_at(k), g_keep, core)
-
+        start(g_send.at[to], g_recv.at[to], gc_s.at[kz], gc_r.at[kz], sibling)
+    for kz in order:
+        partial_rows(zh_at(kz), g_keep, core)
     for k in (1, 2, 3):
         copy(
             dkv.at[0], dkv_recv.at[k], k1_s.at[k], k1_r.at[k], at_zl(k)
@@ -526,40 +643,37 @@
     for k in (1, 2, 3):
         total += dkv_recv[k].astype(F32)
     dkv_all[y, zl] = total.astype(BF16)
-    spot = dkv_all.at[y, zl]
+
+    def quarter(step_y, k):
+        of_y = lax.rem(y + N_Y - step_y, N_Y)
+        return dkv_all.at[of_y, lax.rem(zl + N_ZL - k, N_ZL)]
+
+    def quarter_along_y(k):
+        spot = quarter(0, k)
+        for step in (2, 1, 3):
+            start(spot, spot, k3_s.at[k, step], k3_r.at[k, step], at_y(step))
+
     for k in (1, 2, 3):
+        spot = quarter(0, 0)
         start(spot, spot, k2_s.at[k], k2_r.at[k], at_zl(k))
-
-    for k in order:
-        to = x_at(k)
-        copy(
-            g_send.at[to], g_recv.at[to], gc_s.at[k], gc_r.at[k], sibling
-        ).wait_recv()
-        both = g_keep[to].astype(F32) + g_recv[to].astype(F32)
-        g_keep[to] = both.astype(BF16)
-        if k:
-            for kz in order:
-                to_z = lax.rem(zh + kz, N_ZH)
-                start(
-                    g_keep.at[to, to_z],
-                    x_recv.at[k, to_z],
-                    gx_s.at[k, kz],
-                    gx_r.at[k, kz],
-                    at_x(k),
-                )
-
+    quarter_along_y(0)
+    core_step(2)
+    core_step(1)
+    for k in (1, 2, 3):
+        spot = quarter(0, k)
+        copy(spot, spot, k2_s.at[k], k2_r.at[k], at_zl(k)).wait_recv()
+        quarter_along_y(k)
+    core_step(3)
+    core_step(0)
     line_pass(att_all, a1_s, a1_r, af_s, af_r)
     for k in (1, 3):
         deal(att_all, k, sent_to, att_send, att_slots, a2_s, a2_r)
-
-    for k in (1, 2, 3):
-        copy(spot, spot, k2_s.at[k], k2_r.at[k], at_zl(k)).wait_recv()
-    group = dkv_all.at[y]
-    for k in (1, 2, 3):
-        start(group, group, k3_s.at[k], k3_r.at[k], at_y(k))
-    for k in (1, 2, 3):
-        copy(group, group, k3_s.at[k], k3_r.at[k], at_y(k)).wait_recv()
-
+    for k in range(N_ZL):
+        for step in (1, 2, 3):
+            spot = quarter(step, k)
+            copy(
+                spot, spot, k3_s.at[k, step], k3_r.at[k, step], at_y(step)
+            ).wait_recv()
     for g in range(N_X):
         rows = dkv_all[g].reshape(2 * HEAD, TOKENS)
         product = dot_nt(rows, x_ref[...]).astype(BF16)
@@ -567,44 +681,33 @@
             for i in range(N_ZH):
                 for c in range(N_CORE):
                     first = half * HEAD + i * 32 + c * 16
-                    kv_part[c, g, i, half] = product[first : first + 16]
-    start(kv_part.at[other], kv_recv, vc_s, vc_r, sibling)
-
-    for kz in order:
-        to_z = lax.rem(zh + kz, N_ZH)
-        total = g_keep[x, to_z].astype(F32)
-        for k in (1, 2, 3):
-            spot = x_recv.at[k, to_z]
-            copy(spot, spot, gx_s.at[k, kz], gx_r.at[k, kz], at_x(k)).wait_recv()
-            total += x_recv[k, to_z].astype(F32)
-        z_send[to_z] = total.astype(BF16)
-        if kz:
-            start(
-                z_send.at[to_z], z_recv.at[kz], gz_s.at[kz], gz_r.at[kz], at_zh(kz)
-            )
-
+                    kv_part[c, kv_place(i), g, half] = product[first : first + 16]
+    for part in (0, 1):
+        some = pl.ds(2 * part, 2)
+        start(
+            kv_part.at[other, some],
+            kv_recv.at[some],
+            vc_s.at[part],
+            vc_r.at[part],
+            sibling,
+        )
+    x_step(2)
+    kv_core_step(0)
+    kv_core_step(1)
+    x_step(1)
+    kv_x_step(0)
+    x_step(3)
     line_end(att_all, af_s, af_r)
     deal(att_all, 2, sent_to, att_send, att_slots, a2_s, a2_r)
-    copy(kv_part.at[other], kv_recv, vc_s, vc_r, sibling).wait_recv()
-    kv_sum[...] = (kv_part[core].astype(F32) + kv_recv[...].astype(F32)).astype(BF16)
-    for k in (1, 2, 3):
-        start(kv_sum.at[x_at(k)], kv_x.at[k], vx_s.at[k], vx_r.at[k], at_x(k))
-    total = kv_sum[x].astype(F32)
-    for k in (1, 2, 3):
-        copy(kv_sum.at[0], kv_x.at[k], vx_s.at[k], vx_r.at[k], at_x(k)).wait_recv()
-        total += kv_x[k].astype(F32)
-    kv_zs[...] = total.astype(BF16)
-    for k in (1, 2, 3):
-        to_z = lax.rem(zh + k, N_ZH)
-        start(kv_zs.at[to_z], kv_z.at[k], vz_s.at[k], vz_r.at[k], at_zh(k))
-
+    kv_x_step(1)
+    x_step(0)
     total = z_send[zh].astype(F32)
     for k in (1, 2, 3):
         copy(z_send.at[0], z_recv.at[k], gz_s.at[k], gz_r.at[k], at_zh(k)).wait_recv()
         total += z_recv[k].astype(F32)
     gq_out[...] = total
 
-    total = kv_zs[zh].astype(F32)
+    total = kv_zs[3].astype(F32)
     for k in (1, 2, 3):
         copy(kv_zs.at[0], kv_z.at[k], vz_s.at[k], vz_r.at[k], at_zh(k)).wait_recv()
         total += kv_z[k].astype(F32)
@@ -621,6 +724,16 @@
         att_out[s] = att_slots[place, k]
     for made in sends:
         made.wait_send()
+
+    @pl.when(inner)
+    def _():
+        for args in inner_sends:
+            copy(*args).wait_send()
+
+
+def finish(*refs):
+    for src, dst in zip(refs[:4], refs[4:]):
+        dst[...] = src[...]
 
 
 def local(
@@ -638,14 +751,15 @@
 ):
     dma = pltpu.SemaphoreType.DMA
     vmem = pl.BlockSpec(memory_space=pltpu.VMEM)
-    attended, grad_query, grad_key, grad_value = pl.pallas_call(
+    out_shape = (
+        jax.ShapeDtypeStruct((SEQS, LENGTH, COLS), BF16),
+        jax.ShapeDtypeStruct((HALF, COLS), F32),
+        jax.ShapeDtypeStruct((16, WIDTH), F32),
+        jax.ShapeDtypeStruct((16, WIDTH), F32),
+    )
+    results = pl.pallas_call(
         kernel,
-        out_shape=(
-            jax.ShapeDtypeStruct((SEQS, LENGTH, COLS), BF16),
-            jax.ShapeDtypeStruct((HALF, COLS), F32),
-            jax.ShapeDtypeStruct((16, WIDTH), F32),
-            jax.ShapeDtypeStruct((16, WIDTH), F32),
-        ),
+        out_shape=out_shape,
         in_specs=[pl.BlockSpec(memory_space=pl.ANY)] * 11,
         out_specs=(vmem,) * 4,
         scratch_shapes=[
@@ -691,13 +805,13 @@
             pltpu.VMEM((N_ZL, 64, TOKENS), BF16),
             pltpu.VMEM((N_ZL, 64, TOKENS), BF16),
             pltpu.VMEM((N_Y, N_ZL, 64, TOKENS), BF16),
-            pltpu.VMEM((N_CORE, N_X, N_ZH, 2, 16, PADDED), BF16),
-            pltpu.VMEM((N_X, N_ZH, 2, 16, PADDED), BF16),
+            pltpu.VMEM((N_CORE, N_ZH, N_X, 2, 16, PADDED), BF16),
+            pltpu.VMEM((N_ZH, N_X, 2, 16, PADDED), BF16),
             pltpu.VMEM((N_X, N_ZH, 2, 16, PADDED), BF16),
             pltpu.VMEM((N_X, N_ZH, 2, 16, PADDED), BF16),
             pltpu.VMEM((N_ZH, 2, 16, PADDED), BF16),
             pltpu.VMEM((N_ZH, 2, 16, PADDED), BF16),
-            dma((4,)),
+            dma((5,)),
             dma((4,)),
             dma((4, 2)),
             dma((4, 2)),
@@ -709,14 +823,14 @@
             dma((4,)),
             dma((4,)),
             dma((4,)),
-            dma((2,)),
-            dma((2,)),
+            dma((2, 2)),
+            dma((2, 2)),
             dma((2,)),
             dma((2,)),
             dma,
             dma,
-            dma((2,)),
-            dma((2,)),
+            dma((2, 2)),
+            dma((2, 2)),
             dma((2,)),
             dma((2,)),
             dma,
@@ -725,18 +839,18 @@
             dma((4,)),
             dma((4,)),
             dma((4,)),
-            dma((4,)),
-            dma((4,)),
-            dma((4,)),
-            dma((4,)),
             dma((4, 4)),
             dma((4, 4)),
             dma((4,)),
             dma((4,)),
-            dma,
-            dma,
-            dma((4,)),
-            dma((4,)),
+            dma((4, 4)),
+            dma((4, 4)),
+            dma((4,)),
+            dma((4,)),
+            dma((2,)),
+            dma((2,)),
+            dma((4, 2)),
+            dma((4, 2)),
             dma((4,)),
             dma((4,)),
         ],
@@ -757,6 +871,14 @@
         query_gain.reshape(1, HEAD),
         key_gain.reshape(1, HEAD),
     )
+    attended, grad_query, grad_key, grad_value = pl.pallas_call(
+        finish,
+        out_shape=out_shape,
+        in_specs=[vmem] * 4,
+        out_specs=[vmem] * 4,
+        compiler_params=pltpu.CompilerParams(vmem_limit_bytes=60 * 1024 * 1024),
+        name="results",
+    )(*results)
     return attended, grad_query, grad_key.T, grad_value.T
 
 

time: 125 us -> 113 us (0.904)
  the two profiles are of different devices: /device:TPU:1 before, /device:TPU:70 now
where the time goes in v3:
time: 113 us
  Pallas kernels  112 us (99%)
    pallas_call x1, Pallas kernels, local(): pl.pallas_call(kernel, out_shape=out_shape, in_specs=[pl.BlockSpec(memory...  111 us

profile of v3, /device:TPU:70, one launch (start us, length us, event | category | flops | bytes accessed | tf_op | source)
XLA Modules:
  0.0 113.0 jit_solution(14932438111680185586)
XLA Ops:
  0.6 110.6 %train_step.1 = (bf16[8,32,256]{2,1,0:T(8,128)(2,1)}, f32[160,256]{1,0:T(8,128)}, f32[16,320]{1,0:T(8,128)}, f32[16,320]{1,0:T(8,128)}) custom-call(s32[1,32]{1,0:T(1,128)} %table_in.1, s32[8]{0:T(128)} %source_in.1, s32[8]{0:T(128)} %drawn_in.1, f32[8]{0:T(128)} %weight_in.1, bf16[8,32,320]{2,1,0:T(8,128)(2,1)} %pool_in.1, ...), custom_call_target="tpu_custom_call" | custom-call | tf_op jit(solution)/shard_map/train_step/pallas_call | solution.py:760
  111.3 1.7 %results.1 = (bf16[8,32,256]{2,1,0:T(8,128)(2,1)}, f32[160,256]{1,0:T(8,128)}, f32[16,320]{1,0:T(8,128)}, f32[16,320]{1,0:T(8,128)}) custom-call(bf16[8,32,256]{2,1,0:T(8,128)(2,1)} %get-tuple-element.12.refs_0_, f32[160,256]{1,0:T(8,128)} %get-tuple-element.13.refs_1_, f32[16,320]{1,0:T(8,128)} %get-tuple-element.14.refs_2_, ...), custom_call_target="tpu_custom_call" | custom-call | tf_op jit(solution)/shard_map/results/pallas_call | solution.py:874

commit v4 on v3

--- a/solution.py
+++ b/solution.py
@@ -305,22 +305,23 @@
                     at_zh(step),
                 )
 
+    def line_wait(buf, send, recv, part, then):
+        for way, step in ((0, 1), (1, N_ZH - 1)):
+            some = pl.ds((way ^ part) * half_slots, half_slots)
+            spot = buf[N_ZH - 1 if way == 0 else 1].at[some]
+            copy(
+                spot, spot, send.at[way, part], recv.at[way, part], at_zh(step)
+            ).wait_recv()
+            then(way, step, some, spot)
+
     def line_pass(buf, send, recv, send_on, recv_on):
-        for part in (0, 1):
-            for way, step in ((0, 1), (1, N_ZH - 1)):
-                some = pl.ds((way ^ part) * half_slots, half_slots)
-                spot = buf[N_ZH - 1 if way == 0 else 1].at[some]
-                copy(
-                    spot, spot, send.at[way, part], recv.at[way, part], at_zh(step)
-                ).wait_recv()
-                if part == 0:
-                    start(
-                        spot,
-                        buf[2].at[some],
-                        send_on.at[way],
-                        recv_on.at[way],
-                        at_zh(step),
-                    )
+        def on(way, step, some, spot):
+            start(spot, buf[2].at[some], send_on.at[way], recv_on.at[way], at_zh(step))
+
+        line_wait(buf, send, recv, 0, on)
+
+    def line_rest(buf, send, recv):
+        line_wait(buf, send, recv, 1, lambda *args: None)
 
     def line_end(buf, send_on, recv_on):
         for way in (0, 1):
@@ -420,17 +421,6 @@
     project(mine(3))
     far_arrived(0)
     pass_on(2)
-    w_arrived(1)
-    w_arrived(3)
-    for k in (1, 2):
-        for way in (0, 1):
-            project(near(k, way))
-    pass_on(3)
-    w_arrived(2)
-    for way in (0, 1):
-        project(near(3, way))
-    far_arrived(1)
-    far_arrived(2)
     for k in (1, 2, 3):
         for i, row, rows in ((0, table_row, tables), (1, source_row, sources)):
             copy(
@@ -444,10 +434,25 @@
         fetch.start()
     for fetch in fetches:
         fetch.wait()
+    w_arrived(1)
+    w_arrived(3)
+    for way in (0, 1):
+        project(near(1, way))
+    for way in (0, 1):
+        project(near(2, way))
     line_pass(d_all, c1_s, c1_r, cf_s, cf_r)
+    pass_on(3)
+    w_arrived(2)
+    for way in (0, 1):
+        project(near(3, way))
+    far_arrived(1)
+    far_arrived(2)
+    line_rest(d_all, c1_s, c1_r)
     for k in (1, 3):
         deal(d_all, k, slot_of, d_send, d_slots, c2_s, c2_r)
     far_arrived(3)
+    line_end(d_all, cf_s, cf_r)
+    deal(d_all, 2, slot_of, d_send, d_slots, c2_s, c2_r)
     for k in range(N_X):
         at = lax.rem(x + k, N_X) * SHARE
         spot = w_kv.at[other, :, pl.ds(pl.multiple_of(at, 16), SHARE)]
@@ -488,8 +493,6 @@
     line_send(att_all, a1_s, a1_r)
     deal(att_all, 0, sent_to, att_send, att_slots, a2_s, a2_r)
 
-    line_end(d_all, cf_s, cf_r)
-    deal(d_all, 2, slot_of, d_send, d_slots, c2_s, c2_r)
     dealt(d_slots, c2_s, c2_r)
     lane = lax.broadcasted_iota(jnp.int32, (1, N_DP * LENGTH), 1)
     target = jnp.zeros_like(lane)
@@ -521,9 +524,7 @@
         score_half = (probs * centred * SCALE).astype(BF16)
         d_qnorm = dot_nn(k_norm, score_half)
         d_knorm += dot_nt(q_norm, score_half)
-        d_queries.append(rms_back(query, inverse, gain_q, d_qnorm))
-    for h in range(COLS // HEAD):
-        d_query[:, h * HEAD : (h + 1) * HEAD] = d_queries[h].T.astype(BF16)
+        d_queries.append((query, inverse, gain_q, d_qnorm))
     d_key = rms_back(key_sum, k_inverse, gain_k, d_knorm).astype(BF16)
     d_value = d_value.astype(BF16)
     for q in (0, 1):
@@ -538,6 +539,9 @@
             k1_r.at[k],
             at_zl(k),
         )
+
+    for h in range(COLS // HEAD):
+        d_query[:, h * HEAD : (h + 1) * HEAD] = rms_back(*d_queries[h]).T.astype(BF16)
 
     def x_at(step):
         return lax.rem(x + step, N_X)
@@ -586,22 +590,16 @@
             step == 0, 3, jnp.where(step == 1, 1, jnp.where(step == 2, 0, 2))
         )
 
-    def kv_core_step(part):
-        some = pl.ds(2 * part, 2)
+    def kv_core_step(k):
         copy(
-            kv_part.at[other, some],
-            kv_recv.at[some],
-            vc_s.at[part],
-            vc_r.at[part],
-            sibling,
+            kv_part.at[other, k], kv_recv.at[k], vc_s.at[k], vc_r.at[k], sibling
         ).wait_recv()
-        both = kv_part[core, some].astype(F32) + kv_recv[some].astype(F32)
-        both = both.astype(BF16)
-        for g in range(N_X):
-            kv_sum[g, some] = both[:, g]
-        for k in (2, 1, 3):
+        both = kv_part[core, k].astype(F32) + kv_recv[k].astype(F32)
+        kv_sum[k] = both.astype(BF16)
+        for part in (0, 1) if k else ():
+            some = pl.ds(2 * part, 2)
             start(
-                kv_sum.at[x_at(k), some],
+                kv_sum.at[k, some],
                 kv_x.at[k, some],
                 vx_s.at[k, part],
                 vx_r.at[k, part],
@@ -610,7 +608,7 @@
 
     def kv_x_step(part):
         some = pl.ds(2 * part, 2)
-        total = kv_sum[x, some].astype(F32)
+        total = kv_sum[0, some].astype(F32)
         for k in (1, 2, 3):
             spot = kv_x.at[k, some]
             copy(
@@ -663,42 +661,41 @@
         spot = quarter(0, k)
         copy(spot, spot, k2_s.at[k], k2_r.at[k], at_zl(k)).wait_recv()
         quarter_along_y(k)
+    line_pass(att_all, a1_s, a1_r, af_s, af_r)
     core_step(3)
     core_step(0)
-    line_pass(att_all, a1_s, a1_r, af_s, af_r)
-    for k in (1, 3):
-        deal(att_all, k, sent_to, att_send, att_slots, a2_s, a2_r)
+    x_step(2)
     for k in range(N_ZL):
         for step in (1, 2, 3):
             spot = quarter(step, k)
             copy(
                 spot, spot, k3_s.at[k, step], k3_r.at[k, step], at_y(step)
             ).wait_recv()
-    for g in range(N_X):
-        rows = dkv_all[g].reshape(2 * HEAD, TOKENS)
+    for step in order:
+        rows = dkv_all[x_at(step)].reshape(2 * HEAD, TOKENS)
         product = dot_nt(rows, x_ref[...]).astype(BF16)
         for half in range(2):
             for i in range(N_ZH):
                 for c in range(N_CORE):
                     first = half * HEAD + i * 32 + c * 16
-                    kv_part[c, kv_place(i), g, half] = product[first : first + 16]
-    for part in (0, 1):
-        some = pl.ds(2 * part, 2)
+                    kv_part[c, step, kv_place(i), half] = product[first : first + 16]
         start(
-            kv_part.at[other, some],
-            kv_recv.at[some],
-            vc_s.at[part],
-            vc_r.at[part],
+            kv_part.at[other, step],
+            kv_recv.at[step],
+            vc_s.at[step],
+            vc_r.at[step],
             sibling,
         )
-    x_step(2)
-    kv_core_step(0)
-    kv_core_step(1)
+    line_rest(att_all, a1_s, a1_r)
+    for k in (1, 3):
+        deal(att_all, k, sent_to, att_send, att_slots, a2_s, a2_r)
+    for k in order:
+        kv_core_step(k)
     x_step(1)
-    kv_x_step(0)
-    x_step(3)
     line_end(att_all, af_s, af_r)
     deal(att_all, 2, sent_to, att_send, att_slots, a2_s, a2_r)
+    x_step(3)
+    kv_x_step(0)
     kv_x_step(1)
     x_step(0)
     total = z_send[zh].astype(F32)
@@ -805,8 +802,8 @@
             pltpu.VMEM((N_ZL, 64, TOKENS), BF16),
             pltpu.VMEM((N_ZL, 64, TOKENS), BF16),
             pltpu.VMEM((N_Y, N_ZL, 64, TOKENS), BF16),
-            pltpu.VMEM((N_CORE, N_ZH, N_X, 2, 16, PADDED), BF16),
-            pltpu.VMEM((N_ZH, N_X, 2, 16, PADDED), BF16),
+            pltpu.VMEM((N_CORE, N_X, N_ZH, 2, 16, PADDED), BF16),
+            pltpu.VMEM((N_X, N_ZH, 2, 16, PADDED), BF16),
             pltpu.VMEM((N_X, N_ZH, 2, 16, PADDED), BF16),
             pltpu.VMEM((N_X, N_ZH, 2, 16, PADDED), BF16),
             pltpu.VMEM((N_ZH, 2, 16, PADDED), BF16),
@@ -847,8 +844,8 @@
             dma((4, 4)),
             dma((4,)),
             dma((4,)),
-            dma((2,)),
-            dma((2,)),
+            dma((4,)),
+            dma((4,)),
             dma((4, 2)),
             dma((4, 2)),
             dma((4,)),

time: 113 us -> 110 us (0.973)
  the two profiles are of different devices: /device:TPU:70 before, /device:TPU:2 now
where the time goes in v4:
time: 110 us
  Pallas kernels  109 us (99%)
    pallas_call x1, Pallas kernels, local(): pl.pallas_call(kernel, out_shape=out_shape, in_specs=[pl.BlockSpec(memory...  108 us

profile of v4, /device:TPU:2, one launch (start us, length us, event | category | flops | bytes accessed | tf_op | source)
XLA Modules:
  0.0 110.1 jit_solution(4494247278015061883)
XLA Ops:
  0.6 107.7 %train_step.1 = (bf16[8,32,256]{2,1,0:T(8,128)(2,1)}, f32[160,256]{1,0:T(8,128)}, f32[16,320]{1,0:T(8,128)}, f32[16,320]{1,0:T(8,128)}) custom-call(s32[1,32]{1,0:T(1,128)} %table_in.1, s32[8]{0:T(128)} %source_in.1, s32[8]{0:T(128)} %drawn_in.1, f32[8]{0:T(128)} %weight_in.1, bf16[8,32,320]{2,1,0:T(8,128)(2,1)} %pool_in.1, ...), custom_call_target="tpu_custom_call" | custom-call | tf_op jit(solution)/shard_map/train_step/pallas_call | solution.py:757
  108.3 1.7 %results.1 = (bf16[8,32,256]{2,1,0:T(8,128)(2,1)}, f32[160,256]{1,0:T(8,128)}, f32[16,320]{1,0:T(8,128)}, f32[16,320]{1,0:T(8,128)}) custom-call(bf16[8,32,256]{2,1,0:T(8,128)(2,1)} %get-tuple-element.12.refs_0_, f32[160,256]{1,0:T(8,128)} %get-tuple-element.13.refs_1_, f32[16,320]{1,0:T(8,128)} %get-tuple-element.14.refs_2_, ...), custom_call_target="tpu_custom_call" | custom-call | tf_op jit(solution)/shard_map/results/pallas_call | solution.py:871

commit v5 on v4

--- a/solution.py
+++ b/solution.py
@@ -103,6 +103,7 @@
     x_recv,
     z_send,
     z_recv,
+    z_pass,
     dkv,
     dkv_recv,
     dkv_all,
@@ -146,6 +147,8 @@
     gc_r,
     gx_s,
     gx_r,
+    gp_s,
+    gp_r,
     gz_s,
     gz_r,
     vc_s,
@@ -578,9 +581,28 @@
             spot = x_recv.at[to, k]
             copy(spot, spot, gx_s.at[k, kz], gx_r.at[k, kz], at_x(k)).wait_recv()
             total += x_recv[to, k].astype(F32)
-        z_send[to] = total.astype(BF16)
-        if kz:
-            start(z_send.at[to], z_recv.at[kz], gz_s.at[kz], gz_r.at[kz], at_zh(kz))
+        z_send[kz] = total.astype(BF16)
+        if kz == 2:
+            for way in (1, 3):
+                some = part_for(way)
+                start(
+                    z_send.at[2, some],
+                    z_pass.at[way],
+                    gp_s.at[way],
+                    gp_r.at[way],
+                    at_zh(way),
+                )
+        elif kz:
+            some = part_for(kz)
+            copy(
+                z_pass.at[kz], z_pass.at[kz], gp_s.at[kz], gp_r.at[kz], at_zh(kz)
+            ).wait_recv()
+            both = z_send[kz, some].astype(F32) + z_pass[kz].astype(F32)
+            z_send[kz, some] = both.astype(BF16)
+            start(z_send.at[kz], z_recv.at[kz], gz_s.at[kz], gz_r.at[kz], at_zh(kz))
+
+    def part_for(way):
+        return pl.ds(0 if way == 1 else HALF // 2, HALF // 2)
 
     order = (2, 1, 3, 0)
 
@@ -665,6 +687,9 @@
     core_step(3)
     core_step(0)
     x_step(2)
+    line_rest(att_all, a1_s, a1_r)
+    for k in (1, 3):
+        deal(att_all, k, sent_to, att_send, att_slots, a2_s, a2_r)
     for k in range(N_ZL):
         for step in (1, 2, 3):
             spot = quarter(step, k)
@@ -686,9 +711,6 @@
             vc_r.at[step],
             sibling,
         )
-    line_rest(att_all, a1_s, a1_r)
-    for k in (1, 3):
-        deal(att_all, k, sent_to, att_send, att_slots, a2_s, a2_r)
     for k in order:
         kv_core_step(k)
     x_step(1)
@@ -698,9 +720,10 @@
     kv_x_step(0)
     kv_x_step(1)
     x_step(0)
-    total = z_send[zh].astype(F32)
-    for k in (1, 2, 3):
-        copy(z_send.at[0], z_recv.at[k], gz_s.at[k], gz_r.at[k], at_zh(k)).wait_recv()
+    total = z_send[0].astype(F32)
+    for k in (1, 3):
+        spot = z_recv.at[k]
+        copy(spot, spot, gz_s.at[k], gz_r.at[k], at_zh(k)).wait_recv()
         total += z_recv[k].astype(F32)
     gq_out[...] = total
 
@@ -799,6 +822,7 @@
             pltpu.VMEM((N_X, N_ZH, HALF, COLS), BF16),
             pltpu.VMEM((N_ZH, HALF, COLS), BF16),
             pltpu.VMEM((N_ZH, HALF, COLS), BF16),
+            pltpu.VMEM((N_ZH, HALF // 2, COLS), BF16),
             pltpu.VMEM((N_ZL, 64, TOKENS), BF16),
             pltpu.VMEM((N_ZL, 64, TOKENS), BF16),
             pltpu.VMEM((N_Y, N_ZL, 64, TOKENS), BF16),
@@ -842,6 +866,8 @@
             dma((4,)),
             dma((4, 4)),
             dma((4, 4)),
+            dma((4,)),
+            dma((4,)),
             dma((4,)),
             dma((4,)),
             dma((4,)),

time: 110 us -> 107 us (0.973)
  the two profiles are of different devices: /device:TPU:2 before, /device:TPU:56 now
where the time goes in v5:
time: 107 us
  Pallas kernels  107 us (100%)
    pallas_call x1, Pallas kernels, local(): pl.pallas_call(kernel, out_shape=out_shape, in_specs=[pl.BlockSpec(memory...  105 us

profile of v5, /device:TPU:56, one launch (start us, length us, event | category | flops | bytes accessed | tf_op | source)
XLA Modules:
  0.0 107.3 jit_solution(10917762150891407932)
XLA Ops:
  0.6 105.0 %train_step.1 = (bf16[8,32,256]{2,1,0:T(8,128)(2,1)}, f32[160,256]{1,0:T(8,128)}, f32[16,320]{1,0:T(8,128)}, f32[16,320]{1,0:T(8,128)}) custom-call(s32[1,32]{1,0:T(1,128)} %table_in.1, s32[8]{0:T(128)} %source_in.1, s32[8]{0:T(128)} %drawn_in.1, f32[8]{0:T(128)} %weight_in.1, bf16[8,32,320]{2,1,0:T(8,128)(2,1)} %pool_in.1, ...), custom_call_target="tpu_custom_call" | custom-call | tf_op jit(solution)/shard_map/train_step/pallas_call | solution.py:780
  105.6 1.7 %results.1 = (bf16[8,32,256]{2,1,0:T(8,128)(2,1)}, f32[160,256]{1,0:T(8,128)}, f32[16,320]{1,0:T(8,128)}, f32[16,320]{1,0:T(8,128)}) custom-call(bf16[8,32,256]{2,1,0:T(8,128)(2,1)} %get-tuple-element.12.refs_0_, f32[160,256]{1,0:T(8,128)} %get-tuple-element.13.refs_1_, f32[16,320]{1,0:T(8,128)} %get-tuple-element.14.refs_2_, ...), custom_call_target="tpu_custom_call" | custom-call | tf_op jit(solution)/shard_map/results/pallas_call | solution.py:897

commit v6 on v5

--- a/solution.py
+++ b/solution.py
@@ -698,12 +698,12 @@
             ).wait_recv()
     for step in order:
         rows = dkv_all[x_at(step)].reshape(2 * HEAD, TOKENS)
-        product = dot_nt(rows, x_ref[...]).astype(BF16)
-        for half in range(2):
-            for i in range(N_ZH):
-                for c in range(N_CORE):
-                    first = half * HEAD + i * 32 + c * 16
-                    kv_part[c, step, kv_place(i), half] = product[first : first + 16]
+        product = dot_nt(rows, x_ref[...])[:, :WIDTH]
+        both = jnp.concatenate([product[:HEAD], product[HEAD:]], axis=1).astype(BF16)
+        for i in range(N_ZH):
+            for c in range(N_CORE):
+                first = i * 32 + c * 16
+                kv_part[c, step, kv_place(i)] = both[first : first + 16]
         start(
             kv_part.at[other, step],
             kv_recv.at[step],
@@ -731,8 +731,8 @@
     for k in (1, 2, 3):
         copy(kv_zs.at[0], kv_z.at[k], vz_s.at[k], vz_r.at[k], at_zh(k)).wait_recv()
         total += kv_z[k].astype(F32)
-    gk_out[...] = total[0][:, :WIDTH]
-    gv_out[...] = total[1][:, :WIDTH]
+    gk_out[...] = total[:, :WIDTH]
+    gv_out[...] = total[:, WIDTH:]
 
     dealt(att_slots, a2_s, a2_r)
     for s in range(SEQS):
@@ -826,12 +826,12 @@
             pltpu.VMEM((N_ZL, 64, TOKENS), BF16),
             pltpu.VMEM((N_ZL, 64, TOKENS), BF16),
             pltpu.VMEM((N_Y, N_ZL, 64, TOKENS), BF16),
-            pltpu.VMEM((N_CORE, N_X, N_ZH, 2, 16, PADDED), BF16),
-            pltpu.VMEM((N_X, N_ZH, 2, 16, PADDED), BF16),
-            pltpu.VMEM((N_X, N_ZH, 2, 16, PADDED), BF16),
-            pltpu.VMEM((N_X, N_ZH, 2, 16, PADDED), BF16),
-            pltpu.VMEM((N_ZH, 2, 16, PADDED), BF16),
-            pltpu.VMEM((N_ZH, 2, 16, PADDED), BF16),
+            pltpu.VMEM((N_CORE, N_X, N_ZH, 16, 2 * WIDTH), BF16),
+            pltpu.VMEM((N_X, N_ZH, 16, 2 * WIDTH), BF16),
+            pltpu.VMEM((N_X, N_ZH, 16, 2 * WIDTH), BF16),
+            pltpu.VMEM((N_X, N_ZH, 16, 2 * WIDTH), BF16),
+            pltpu.VMEM((N_ZH, 16, 2 * WIDTH), BF16),
+            pltpu.VMEM((N_ZH, 16, 2 * WIDTH), BF16),
             dma((5,)),
             dma((4,)),
             dma((4, 2)),

time: 107 us -> 107 us (level)
  the two profiles are of different devices: /device:TPU:56 before, /device:TPU:17 now
where the time goes in v6:
time: 107 us
  Pallas kernels  106 us (99%)
    pallas_call x1, Pallas kernels, local(): pl.pallas_call(kernel, out_shape=out_shape, in_specs=[pl.BlockSpec(memory...  105 us

profile of v6, /device:TPU:17, one launch (start us, length us, event | category | flops | bytes accessed | tf_op | source)
XLA Modules:
  0.0 107.0 jit_solution(7789386418308577095)
XLA Ops:
  0.6 104.6 %train_step.1 = (bf16[8,32,256]{2,1,0:T(8,128)(2,1)}, f32[160,256]{1,0:T(8,128)}, f32[16,320]{1,0:T(8,128)}, f32[16,320]{1,0:T(8,128)}) custom-call(s32[1,32]{1,0:T(1,128)} %table_in.1, s32[8]{0:T(128)} %source_in.1, s32[8]{0:T(128)} %drawn_in.1, f32[8]{0:T(128)} %weight_in.1, bf16[8,32,320]{2,1,0:T(8,128)(2,1)} %pool_in.1, ...), custom_call_target="tpu_custom_call" | custom-call | tf_op jit(solution)/shard_map/train_step/pallas_call | solution.py:780
  105.2 1.7 %results.1 = (bf16[8,32,256]{2,1,0:T(8,128)(2,1)}, f32[160,256]{1,0:T(8,128)}, f32[16,320]{1,0:T(8,128)}, f32[16,320]{1,0:T(8,128)}) custom-call(bf16[8,32,256]{2,1,0:T(8,128)(2,1)} %get-tuple-element.12.refs_0_, f32[160,256]{1,0:T(8,128)} %get-tuple-element.13.refs_1_, f32[16,320]{1,0:T(8,128)} %get-tuple-element.14.refs_2_, ...), custom_call_target="tpu_custom_call" | custom-call | tf_op jit(solution)/shard_map/results/pallas_call | solution.py:897
